TPU v7x, 512 devices: a whole 4x4x16 slice. The times are simulated.
512 devices in a mesh: chan: 32 (over z, core), seq: 16 (over x, y).
Axes of the slice: x: 4, y: 4, z: 16, core: 2. Of those that a mesh axis runs over, the one named last changes fastest.
Arguments:
- features: bfloat16 [3, 32768, 4096], P(None, ('seq', 'chan')), may hold values from -6 to 6
- short_taps: float32 [3, 3, 4096], replicated, may hold values from -3 to 3
- decay_rates: float32 [16, 4096], P(None, 'chan'), may hold values from 3.0517579e-06 to 0.03
- residues: float32 [16, 4096], P(None, 'chan'), may hold values from -1.5 to 1.5
- skip_gain: float32 [4096], P('chan'), may hold values from -3 to 3
Outputs:
- gated_out: bfloat16 [32768, 4096], P(('seq', 'chan'))
All inputs are finite; a program needn't handle non-finite values.
Results may differ from a plain program's by a relative error of at most 0.0058.
Values may be sent and summed in bfloat16 or wider, within the bound.
A program may use at most 64 MiB of HBM per device.

v0:
```python
import jax
import jax.numpy as jnp
from jax import lax
from jax.sharding import PartitionSpec as P


def from_behind(block, axis, distance):
    devices = range(lax.axis_size(axis))
    route = [(i - distance, i) for i in devices if i - distance in devices]
    return lax.ppermute(block, axis, route)


def filter_tables(decay_rates, residues, sub_len):
    offsets = jnp.arange(sub_len).astype(decay_rates.dtype)
    powers = jnp.exp(-decay_rates[:, None, :] * offsets[None, :, None])
    weighted = residues * jnp.sqrt(-jnp.expm1(-2.0 * decay_rates))
    impulse = jnp.sum(weighted[:, None, :] * powers, axis=0)
    lag_index = jnp.arange(sub_len)[:, None] - jnp.arange(sub_len)[None, :]
    picked = jnp.take(impulse, jnp.maximum(lag_index, 0), axis=0)
    toeplitz = jnp.where((lag_index >= 0)[:, :, None], picked, jnp.zeros_like(picked))
    entry_weight = powers[:, ::-1, :]
    reach_weight = weighted[:, None, :] * powers * jnp.exp(-decay_rates)[:, None, :]
    return (toeplitz, entry_weight, reach_weight)


def short_mix(padded, short_taps):
    count = short_taps.shape[1]
    row_count = padded.shape[1] - (count - 1)
    widened = padded.astype(jnp.float32)
    filtered = jnp.zeros((3, row_count, padded.shape[2]), jnp.float32)
    for shift_by in range(count):
        start_row = count - 1 - shift_by
        filtered = (
            filtered
            + short_taps[:, shift_by][:, None, :] * widened[:, start_row : start_row + row_count, :]
        )
    gating = filtered[0].astype(jnp.bfloat16)
    product = (filtered[1] * filtered[2]).astype(jnp.bfloat16)
    return (gating, product)


def per_device(features, short_taps, decay_rates, residues, skip_gain):
    channels = decay_rates.shape[1]
    edge_width = short_taps.shape[1] - 1
    exchanged = lax.all_to_all(features, "chan", split_axis=2, concat_axis=1, tiled=True)
    edge_rows = exchanged[:, exchanged.shape[1] - edge_width :, :]
    earlier = from_behind(edge_rows, "seq", 1)
    offset = lax.axis_index("chan") * channels
    local_taps = lax.dynamic_slice_in_dim(short_taps, offset, channels, 2)
    gating, product = short_mix(jnp.concatenate([earlier, exchanged], axis=1), local_taps)
    block_len = gating.shape[0]
    sub_len = min(128, block_len)
    sub_count = block_len // sub_len
    highest = lax.Precision.HIGHEST
    toeplitz, entry_weight, reach_weight = filter_tables(decay_rates, residues, sub_len)
    z_values = product.astype(jnp.float32).reshape(sub_count, sub_len, channels)
    inner_part = jnp.einsum("tsc,bsc->btc", toeplitz, z_values, precision=highest)
    end_states = jnp.einsum("msc,bsc->bmc", entry_weight, z_values, precision=highest)
    step_decay = jnp.exp(-decay_rates * sub_len)

    def advance(state_in, end_state):
        return (step_decay * state_in + end_state, state_in)

    zero_state = jnp.zeros((decay_rates.shape[0], channels), jnp.float32)
    local_end, prefixes = lax.scan(advance, zero_state, end_states)
    block_decay = jnp.exp(-decay_rates * block_len)

    def relay_turn(counter, incoming_state):
        return from_behind(block_decay * incoming_state + local_end, "seq", 1)

    incoming = lax.fori_loop(0, lax.axis_size("seq") - 1, relay_turn, zero_state)
    sub_offsets = (jnp.arange(sub_count) * sub_len).astype(jnp.float32)
    carried = jnp.exp(-decay_rates[None, :, :] * sub_offsets[:, None, None]) * incoming[None, :, :]
    start_states = prefixes + carried
    cross_part = jnp.einsum("mtc,bmc->btc", reach_weight, start_states, precision=highest)
    convolved = (inner_part + cross_part).reshape(block_len, channels)
    result = gating.astype(jnp.float32) * (
        convolved + skip_gain[None, :] * product.astype(jnp.float32)
    )
    return lax.all_to_all(
        result.astype(jnp.bfloat16), "chan", split_axis=0, concat_axis=1, tiled=True
    )


def solution(mesh):
    placed = (P(None, ("seq", "chan"), None), P(), P(None, "chan"), P(None, "chan"), P("chan"))
    return jax.shard_map(
        per_device, mesh=mesh, in_specs=placed, out_specs=P(("seq", "chan"), None), check_vma=False
    )
```

profile of v0, /device:TPU:7, one launch (start us, length us, event | category | flops | bytes accessed | tf_op | source)
XLA Modules:
  0.0 359.1 jit_solution(14924009756692679859)
XLA Ops:
  0.0 6.4 %copy.33 = bf16[3,64,4096]{1,0,2:T(4,128)(2,1)} copy(bf16[3,64,4096]{2,1,0:T(8,128)(2,1)} %param.9) | data formatting | bytes 3145728 | tf_op args[0]
  6.4 7.3 %reshape.99 = bf16[32,2,12288]{2,1,0:T(2,128)(2,1)} reshape(bf16[4096,3,64]{2,1,0:T(4,128)(2,1)} %bitcast.47) | data formatting | bytes 3145728
  13.7 15.9 %all-to-all-start = ((bf16[32,2,12288]{2,1,0:T(2,128)(2,1)}), bf16[32,2,12288]{2,1,0:T(2,128)(2,1)S(1)}, u32[]{:S(2)}, u32[]{:S(2)}) async-start(bf16[32,2,12288]{2,1,0:T(2,128)(2,1)} %reshape.99), calls=%async_computation | async-start | bytes 3145728 | tf_op jit(solution)/shard_map/all_to_all | solution.py:45
  29.7 0.1 copy.36
  29.8 0.1 copy.37
  29.9 0.9 constant_dynamic-slice_fusion.1
  30.8 1.6 multiply_exponential_fusion
  32.4 75.0 %all-to-all-done = bf16[32,2,12288]{2,1,0:T(2,128)(2,1)S(1)} async-done(((bf16[32,2,12288]{2,1,0:T(2,128)(2,1)}), bf16[32,2,12288]{2,1,0:T(2,128)(2,1)S(1)}, u32[]{:S(2)}, u32[]{:S(2)}) %all-to-all-start) | async-done | bytes 1572896 | tf_op jit(solution)/shard_map/all_to_all | solution.py:45
  107.4 4.8 %reshape.100 = bf16[4096,3,64]{2,1,0:T(4,128)(2,1)} reshape(bf16[32,2,12288]{2,1,0:T(2,128)(2,1)S(1)} %all-to-all-done) | data formatting | bytes 3145728
  112.2 5.8 %copy.48 = bf16[3,64,32,128]{3,1,2,0:T(8,128)(2,1)S(1)} copy(bf16[3,64,32,128]{1,0,3,2:T(4,128)(2,1)} %bitcast.46) | data formatting | bytes 3145728 | tf_op jit(solution)/shard_map/all_to_all | solution.py:45
  118.0 3.4 collective-permute-start.1
  121.4 0.1 copy.43
  121.5 1.5 rev.3
  123.0 0.1 copy.38
  123.1 54.8 %gather_fusion = f32[16384,128]{1,0:T(8,128)} fusion(f32[128,128]{1,0:T(8,128)S(1)} %copy.38, s32[16384]{0:T(1024)S(1)} %bitcast_clamp_fusion), kind=kCustom, calls=%fused_computation | custom fusion | bytes 16842752 | tf_op jit(solution)/shard_map/jit(_take)/gather | solution.py:19
  177.9 9.4 %copy.39 = f32[128,128,128]{1,0,2:T(8,128)} copy(f32[128,128,128]{2,1,0:T(8,128)} %bitcast.45) | data formatting | bytes 16777216 | tf_op jit(solution)/shard_map/jit(_take)/gather | solution.py:19
  187.3 0.3 maximum_convert_fusion
  187.6 0.9 fusion.7
  188.5 0.1 fusion.10
  188.6 0.8 slice.66
  189.5 0.4 copy.40
  189.9 2.0 convolution_bitcast_fusion
  191.9 1.6 copy.42
  193.5 0.8 while.24
  194.3 97.7 %while.23 = (s32[]{:T(128)}, f32[16,128]{1,0:T(8,128)S(1)}, f32[16,128]{1,0:T(8,128)S(1)}, f32[16,128]{1,0:T(8,128)S(1)}, s32[]{:T(128)}) while((s32[]{:T(128)}, f32[16,128]{1,0:T(8,128)S(1)}, f32[16,128]{1,0:T(8,128)S(1)}, f32[16,128]{1,0:T(8,128)S(1)}, s32[]{:T(128)}) %tuple.51), condition=%wide.region_4.5_spmd, body=%wide.region_3.4_spmd.sunk | while | flops 4098 | bytes 65637 | solution.py:71
  194.3 3.2 collective-permute-start
  197.5 3.3 collective-permute-done
  200.8 1.9 collective-permute-start
  202.7 4.6 %collective-permute-done = f32[16,128]{1,0:T(8,128)S(1)} collective-permute-done((f32[16,128]{1,0:T(8,128)S(1)}, f32[16,128]{1,0:T(8,128)S(1)}, u32[]{:S(2)}, u32[]{:S(2)}) %collective-permute-start) | collective-permute-done | bytes 8224 | tf_op jit(solution)/shard_map/while/body/eval_jaxpr/ppermute | solution.py:10
  207.3 1.9 collective-permute-start
  209.2 4.6 %collective-permute-done = f32[16,128]{1,0:T(8,128)S(1)} collective-permute-done((f32[16,128]{1,0:T(8,128)S(1)}, f32[16,128]{1,0:T(8,128)S(1)}, u32[]{:S(2)}, u32[]{:S(2)}) %collective-permute-start) | collective-permute-done | bytes 8224 | tf_op jit(solution)/shard_map/while/body/eval_jaxpr/ppermute | solution.py:10
  213.8 1.9 collective-permute-start
  215.7 4.6 %collective-permute-done = f32[16,128]{1,0:T(8,128)S(1)} collective-permute-done((f32[16,128]{1,0:T(8,128)S(1)}, f32[16,128]{1,0:T(8,128)S(1)}, u32[]{:S(2)}, u32[]{:S(2)}) %collective-permute-start) | collective-permute-done | bytes 8224 | tf_op jit(solution)/shard_map/while/body/eval_jaxpr/ppermute | solution.py:10
  220.3 1.9 collective-permute-start
  222.2 4.6 %collective-permute-done = f32[16,128]{1,0:T(8,128)S(1)} collective-permute-done((f32[16,128]{1,0:T(8,128)S(1)}, f32[16,128]{1,0:T(8,128)S(1)}, u32[]{:S(2)}, u32[]{:S(2)}) %collective-permute-start) | collective-permute-done | bytes 8224 | tf_op jit(solution)/shard_map/while/body/eval_jaxpr/ppermute | solution.py:10
  226.8 1.9 collective-permute-start
  228.7 4.6 %collective-permute-done = f32[16,128]{1,0:T(8,128)S(1)} collective-permute-done((f32[16,128]{1,0:T(8,128)S(1)}, f32[16,128]{1,0:T(8,128)S(1)}, u32[]{:S(2)}, u32[]{:S(2)}) %collective-permute-start) | collective-permute-done | bytes 8224 | tf_op jit(solution)/shard_map/while/body/eval_jaxpr/ppermute | solution.py:10
  233.3 1.9 collective-permute-start
  235.2 4.6 %collective-permute-done = f32[16,128]{1,0:T(8,128)S(1)} collective-permute-done((f32[16,128]{1,0:T(8,128)S(1)}, f32[16,128]{1,0:T(8,128)S(1)}, u32[]{:S(2)}, u32[]{:S(2)}) %collective-permute-start) | collective-permute-done | bytes 8224 | tf_op jit(solution)/shard_map/while/body/eval_jaxpr/ppermute | solution.py:10
  239.8 1.9 collective-permute-start
  241.7 4.6 %collective-permute-done = f32[16,128]{1,0:T(8,128)S(1)} collective-permute-done((f32[16,128]{1,0:T(8,128)S(1)}, f32[16,128]{1,0:T(8,128)S(1)}, u32[]{:S(2)}, u32[]{:S(2)}) %collective-permute-start) | collective-permute-done | bytes 8224 | tf_op jit(solution)/shard_map/while/body/eval_jaxpr/ppermute | solution.py:10
  246.3 1.9 collective-permute-start
  248.2 4.6 %collective-permute-done = f32[16,128]{1,0:T(8,128)S(1)} collective-permute-done((f32[16,128]{1,0:T(8,128)S(1)}, f32[16,128]{1,0:T(8,128)S(1)}, u32[]{:S(2)}, u32[]{:S(2)}) %collective-permute-start) | collective-permute-done | bytes 8224 | tf_op jit(solution)/shard_map/while/body/eval_jaxpr/ppermute | solution.py:10
  252.8 1.9 collective-permute-start
  254.7 4.6 %collective-permute-done = f32[16,128]{1,0:T(8,128)S(1)} collective-permute-done((f32[16,128]{1,0:T(8,128)S(1)}, f32[16,128]{1,0:T(8,128)S(1)}, u32[]{:S(2)}, u32[]{:S(2)}) %collective-permute-start) | collective-permute-done | bytes 8224 | tf_op jit(solution)/shard_map/while/body/eval_jaxpr/ppermute | solution.py:10
  259.3 1.9 collective-permute-start
  261.2 4.6 %collective-permute-done = f32[16,128]{1,0:T(8,128)S(1)} collective-permute-done((f32[16,128]{1,0:T(8,128)S(1)}, f32[16,128]{1,0:T(8,128)S(1)}, u32[]{:S(2)}, u32[]{:S(2)}) %collective-permute-start) | collective-permute-done | bytes 8224 | tf_op jit(solution)/shard_map/while/body/eval_jaxpr/ppermute | solution.py:10
  265.8 1.9 collective-permute-start
  267.7 4.6 %collective-permute-done = f32[16,128]{1,0:T(8,128)S(1)} collective-permute-done((f32[16,128]{1,0:T(8,128)S(1)}, f32[16,128]{1,0:T(8,128)S(1)}, u32[]{:S(2)}, u32[]{:S(2)}) %collective-permute-start) | collective-permute-done | bytes 8224 | tf_op jit(solution)/shard_map/while/body/eval_jaxpr/ppermute | solution.py:10
  272.3 1.9 collective-permute-start
  274.2 4.7 %collective-permute-done = f32[16,128]{1,0:T(8,128)S(1)} collective-permute-done((f32[16,128]{1,0:T(8,128)S(1)}, f32[16,128]{1,0:T(8,128)S(1)}, u32[]{:S(2)}, u32[]{:S(2)}) %collective-permute-start) | collective-permute-done | bytes 8224 | tf_op jit(solution)/shard_map/while/body/eval_jaxpr/ppermute | solution.py:10
  279.0 1.9 collective-permute-start
  280.9 4.6 %collective-permute-done = f32[16,128]{1,0:T(8,128)S(1)} collective-permute-done((f32[16,128]{1,0:T(8,128)S(1)}, f32[16,128]{1,0:T(8,128)S(1)}, u32[]{:S(2)}, u32[]{:S(2)}) %collective-permute-start) | collective-permute-done | bytes 8224 | tf_op jit(solution)/shard_map/while/body/eval_jaxpr/ppermute | solution.py:10
  285.5 1.9 collective-permute-start
  287.4 4.6 %collective-permute-done = f32[16,128]{1,0:T(8,128)S(1)} collective-permute-done((f32[16,128]{1,0:T(8,128)S(1)}, f32[16,128]{1,0:T(8,128)S(1)}, u32[]{:S(2)}, u32[]{:S(2)}) %collective-permute-start) | collective-permute-done | bytes 8224 | tf_op jit(solution)/shard_map/while/body/eval_jaxpr/ppermute | solution.py:10
  291.9 0.1 multiply_add_fusion.1
  292.0 0.5 copy.44
  292.5 9.0 %fusion = f32[128,16,128]{2,1,0:T(8,128)S(1)} fusion(bf16[16,128,128]{1,0,2:T(8,128)(2,1)S(1)} %copy.40, f32[128,128,128]{1,0,2:T(8,128)} %copy.39, pred[128,128]{1,0:T(8,128)(4,1)S(1)} %get-tuple-element.126, pred[128,128]{1,0:T(8,128)(4,1)S(1)} %get-tuple-element.127), kind=kOutput, calls=%fused_computation.4 | convolution fusion | flops 406847488 | bytes 9994240 | tf_op jit(solution)/shard_map/tsc,bsc->btc/dot_general | solution.py:57
  301.6 0.0 copy-start.3
  301.6 1.7 fusion.9
  303.3 0.4 copy.45
  303.8 0.2 fusion.13
  304.0 54.2 %all_to_all.34 = bf16[32,64,128]{2,1,0:T(8,128)(2,1)S(1)} all-to-all(bf16[32,64,128]{2,1,0:T(8,128)(2,1)S(1)} %fusion.13), channel_id=1, replica_groups=mesh['chan'=32,'seq'=16] {'chan'}, dimensions={0} | all-to-all | bytes 1048576 | tf_op jit(solution)/shard_map/all_to_all | solution.py:80
  358.2 0.9 copy_bitcast_fusion
  (66 shorter events, 0.5 us)
Async XLA Ops:
  6.4 23.2 %copy-start.1 = (f32[16,128]{1,0:T(8,128)S(1)}, f32[16,128]{1,0:T(8,128)}, u32[]{:S(2)}) copy-start(f32[16,128]{1,0:T(8,128)} %param.11) | copy-start | bytes 24580
  6.4 23.2 %copy-start.2 = (f32[16,128]{1,0:T(8,128)S(1)}, f32[16,128]{1,0:T(8,128)}, u32[]{:S(2)}) copy-start(f32[16,128]{1,0:T(8,128)} %param.12) | copy-start | bytes 24580
  13.7 93.8 %all-to-all-start = ((bf16[32,2,12288]{2,1,0:T(2,128)(2,1)}), bf16[32,2,12288]{2,1,0:T(2,128)(2,1)S(1)}, u32[]{:S(2)}, u32[]{:S(2)}) async-start(bf16[32,2,12288]{2,1,0:T(2,128)(2,1)} %reshape.99), calls=%async_computation | async-start | bytes 3145728 | tf_op jit(solution)/shard_map/all_to_all | solution.py:45
  118.0 69.3 %collective-permute-start.1 = (bf16[3,2,128]{2,1,0:T(2,128)(2,1)S(1)}, bf16[3,2,128]{2,1,0:T(2,128)(2,1)S(1)}, u32[]{:S(2)}, u32[]{:S(2)}) collective-permute-start(bf16[3,2,128]{2,1,0:T(2,128)(2,1)S(1)} %slice.43), channel_id=1, source_target_pairs={{0,1},{1,2},{2,3},{3,4},{4,5},{5,6},{6,7},{7,8},{8,9},{9,10},{10,1... | collective-permute-start | bytes 4616 | tf_op jit(solution)/shard_map/ppermute | solution.py:10
  194.3 6.5 %collective-permute-start = (f32[16,128]{1,0:T(8,128)S(1)}, f32[16,128]{1,0:T(8,128)S(1)}, u32[]{:S(2)}, u32[]{:S(2)}) collective-permute-start(f32[16,128]{1,0:T(8,128)S(1)} %multiply_add_fusion.3), channel_id=1, source_target_pairs={{0,1},{1,2},{2,3},{3,4},{4,5},{5,6},{6,7},{7,8},{8,9},{9,10},{10,1... | collective-permute-start | bytes 24584 | tf_op jit(solution)/shard_map/while/body/eval_jaxpr/ppermute | solution.py:10
  200.8 6.5 %collective-permute-start = (f32[16,128]{1,0:T(8,128)S(1)}, f32[16,128]{1,0:T(8,128)S(1)}, u32[]{:S(2)}, u32[]{:S(2)}) collective-permute-start(f32[16,128]{1,0:T(8,128)S(1)} %multiply_add_fusion.3), channel_id=1, source_target_pairs={{0,1},{1,2},{2,3},{3,4},{4,5},{5,6},{6,7},{7,8},{8,9},{9,10},{10,1... | collective-permute-start | bytes 24584 | tf_op jit(solution)/shard_map/while/body/eval_jaxpr/ppermute | solution.py:10
  207.3 6.5 %collective-permute-start = (f32[16,128]{1,0:T(8,128)S(1)}, f32[16,128]{1,0:T(8,128)S(1)}, u32[]{:S(2)}, u32[]{:S(2)}) collective-permute-start(f32[16,128]{1,0:T(8,128)S(1)} %multiply_add_fusion.3), channel_id=1, source_target_pairs={{0,1},{1,2},{2,3},{3,4},{4,5},{5,6},{6,7},{7,8},{8,9},{9,10},{10,1... | collective-permute-start | bytes 24584 | tf_op jit(solution)/shard_map/while/body/eval_jaxpr/ppermute | solution.py:10
  213.8 6.5 %collective-permute-start = (f32[16,128]{1,0:T(8,128)S(1)}, f32[16,128]{1,0:T(8,128)S(1)}, u32[]{:S(2)}, u32[]{:S(2)}) collective-permute-start(f32[16,128]{1,0:T(8,128)S(1)} %multiply_add_fusion.3), channel_id=1, source_target_pairs={{0,1},{1,2},{2,3},{3,4},{4,5},{5,6},{6,7},{7,8},{8,9},{9,10},{10,1... | collective-permute-start | bytes 24584 | tf_op jit(solution)/shard_map/while/body/eval_jaxpr/ppermute | solution.py:10
  220.3 6.5 %collective-permute-start = (f32[16,128]{1,0:T(8,128)S(1)}, f32[16,128]{1,0:T(8,128)S(1)}, u32[]{:S(2)}, u32[]{:S(2)}) collective-permute-start(f32[16,128]{1,0:T(8,128)S(1)} %multiply_add_fusion.3), channel_id=1, source_target_pairs={{0,1},{1,2},{2,3},{3,4},{4,5},{5,6},{6,7},{7,8},{8,9},{9,10},{10,1... | collective-permute-start | bytes 24584 | tf_op jit(solution)/shard_map/while/body/eval_jaxpr/ppermute | solution.py:10
  226.8 6.5 %collective-permute-start = (f32[16,128]{1,0:T(8,128)S(1)}, f32[16,128]{1,0:T(8,128)S(1)}, u32[]{:S(2)}, u32[]{:S(2)}) collective-permute-start(f32[16,128]{1,0:T(8,128)S(1)} %multiply_add_fusion.3), channel_id=1, source_target_pairs={{0,1},{1,2},{2,3},{3,4},{4,5},{5,6},{6,7},{7,8},{8,9},{9,10},{10,1... | collective-permute-start | bytes 24584 | tf_op jit(solution)/shard_map/while/body/eval_jaxpr/ppermute | solution.py:10
  233.3 6.5 %collective-permute-start = (f32[16,128]{1,0:T(8,128)S(1)}, f32[16,128]{1,0:T(8,128)S(1)}, u32[]{:S(2)}, u32[]{:S(2)}) collective-permute-start(f32[16,128]{1,0:T(8,128)S(1)} %multiply_add_fusion.3), channel_id=1, source_target_pairs={{0,1},{1,2},{2,3},{3,4},{4,5},{5,6},{6,7},{7,8},{8,9},{9,10},{10,1... | collective-permute-start | bytes 24584 | tf_op jit(solution)/shard_map/while/body/eval_jaxpr/ppermute | solution.py:10
  239.8 6.5 %collective-permute-start = (f32[16,128]{1,0:T(8,128)S(1)}, f32[16,128]{1,0:T(8,128)S(1)}, u32[]{:S(2)}, u32[]{:S(2)}) collective-permute-start(f32[16,128]{1,0:T(8,128)S(1)} %multiply_add_fusion.3), channel_id=1, source_target_pairs={{0,1},{1,2},{2,3},{3,4},{4,5},{5,6},{6,7},{7,8},{8,9},{9,10},{10,1... | collective-permute-start | bytes 24584 | tf_op jit(solution)/shard_map/while/body/eval_jaxpr/ppermute | solution.py:10
  246.3 6.5 %collective-permute-start = (f32[16,128]{1,0:T(8,128)S(1)}, f32[16,128]{1,0:T(8,128)S(1)}, u32[]{:S(2)}, u32[]{:S(2)}) collective-permute-start(f32[16,128]{1,0:T(8,128)S(1)} %multiply_add_fusion.3), channel_id=1, source_target_pairs={{0,1},{1,2},{2,3},{3,4},{4,5},{5,6},{6,7},{7,8},{8,9},{9,10},{10,1... | collective-permute-start | bytes 24584 | tf_op jit(solution)/shard_map/while/body/eval_jaxpr/ppermute | solution.py:10
  252.8 6.5 %collective-permute-start = (f32[16,128]{1,0:T(8,128)S(1)}, f32[16,128]{1,0:T(8,128)S(1)}, u32[]{:S(2)}, u32[]{:S(2)}) collective-permute-start(f32[16,128]{1,0:T(8,128)S(1)} %multiply_add_fusion.3), channel_id=1, source_target_pairs={{0,1},{1,2},{2,3},{3,4},{4,5},{5,6},{6,7},{7,8},{8,9},{9,10},{10,1... | collective-permute-start | bytes 24584 | tf_op jit(solution)/shard_map/while/body/eval_jaxpr/ppermute | solution.py:10
  259.3 6.5 %collective-permute-start = (f32[16,128]{1,0:T(8,128)S(1)}, f32[16,128]{1,0:T(8,128)S(1)}, u32[]{:S(2)}, u32[]{:S(2)}) collective-permute-start(f32[16,128]{1,0:T(8,128)S(1)} %multiply_add_fusion.3), channel_id=1, source_target_pairs={{0,1},{1,2},{2,3},{3,4},{4,5},{5,6},{6,7},{7,8},{8,9},{9,10},{10,1... | collective-permute-start | bytes 24584 | tf_op jit(solution)/shard_map/while/body/eval_jaxpr/ppermute | solution.py:10
  265.8 6.5 %collective-permute-start = (f32[16,128]{1,0:T(8,128)S(1)}, f32[16,128]{1,0:T(8,128)S(1)}, u32[]{:S(2)}, u32[]{:S(2)}) collective-permute-start(f32[16,128]{1,0:T(8,128)S(1)} %multiply_add_fusion.3), channel_id=1, source_target_pairs={{0,1},{1,2},{2,3},{3,4},{4,5},{5,6},{6,7},{7,8},{8,9},{9,10},{10,1... | collective-permute-start | bytes 24584 | tf_op jit(solution)/shard_map/while/body/eval_jaxpr/ppermute | solution.py:10
  272.3 6.6 %collective-permute-start = (f32[16,128]{1,0:T(8,128)S(1)}, f32[16,128]{1,0:T(8,128)S(1)}, u32[]{:S(2)}, u32[]{:S(2)}) collective-permute-start(f32[16,128]{1,0:T(8,128)S(1)} %multiply_add_fusion.3), channel_id=1, source_target_pairs={{0,1},{1,2},{2,3},{3,4},{4,5},{5,6},{6,7},{7,8},{8,9},{9,10},{10,1... | collective-permute-start | bytes 24584 | tf_op jit(solution)/shard_map/while/body/eval_jaxpr/ppermute | solution.py:10
  279.0 6.5 %collective-permute-start = (f32[16,128]{1,0:T(8,128)S(1)}, f32[16,128]{1,0:T(8,128)S(1)}, u32[]{:S(2)}, u32[]{:S(2)}) collective-permute-start(f32[16,128]{1,0:T(8,128)S(1)} %multiply_add_fusion.3), channel_id=1, source_target_pairs={{0,1},{1,2},{2,3},{3,4},{4,5},{5,6},{6,7},{7,8},{8,9},{9,10},{10,1... | collective-permute-start | bytes 24584 | tf_op jit(solution)/shard_map/while/body/eval_jaxpr/ppermute | solution.py:10
  285.5 6.5 %collective-permute-start = (f32[16,128]{1,0:T(8,128)S(1)}, f32[16,128]{1,0:T(8,128)S(1)}, u32[]{:S(2)}, u32[]{:S(2)}) collective-permute-start(f32[16,128]{1,0:T(8,128)S(1)} %multiply_add_fusion.3), channel_id=1, source_target_pairs={{0,1},{1,2},{2,3},{3,4},{4,5},{5,6},{6,7},{7,8},{8,9},{9,10},{10,1... | collective-permute-start | bytes 24584 | tf_op jit(solution)/shard_map/while/body/eval_jaxpr/ppermute | solution.py:10
  301.6 2.2 copy-start
  301.6 2.2 copy-start.3
where the time goes:
time: 361 us; the launch traced here: 359 us
  waiting for transfers between devices  142 us (39%)
  local copies, waits for them, and re-layouts  95.8 us (27%)
  blocking collectives  54.2 us (15%)
  starting transfers between devices  49.2 us (14%)
  matrix products  12.8 us (4%)
  other arithmetic  3.7 us (1%)
    all_to_all x1, waiting for transfers between devices, per_device(): lax.all_to_all(features, 'chan', split_axis=2, concat_axis=1, tiled=True)  75 us
    ppermute x16, waiting for transfers between devices, from_behind(): return lax.ppermute(block, axis, route)  67.5 us
    gather x2, local copies, waits for them, and re-layouts, filter_tables(): picked = jnp.take(impulse, jnp.maximum(lag_index, 0), axis=0)  64.2 us
    all_to_all x1, blocking collectives, per_device(): lax.all_to_all(result.astype(jnp.bfloat16), 'chan', split_axis=0, concat_...  54.2 us
    ppermute x16, starting transfers between devices, from_behind(): return lax.ppermute(block, axis, route)  33.3 us
    unnamed x14, local copies, waits for them, and re-layouts  20 us
    all_to_all x1, starting transfers between devices, per_device(): lax.all_to_all(features, 'chan', split_axis=2, concat_axis=1, tiled=True)  15.9 us
    dot_general x1, matrix products, per_device(): jnp.einsum('tsc,bsc->btc', toeplitz, z_values, precision=highest)  9.03 us
  transfers between devices with their start and end apart: 17, of which 16 were waited for; matrix products, arithmetic and copies ran while one was open for 19% of the time, Pallas kernels for 0%

commit v1 on v0

v1 whole, which is shorter than its diff:
```python
import functools

import jax
import jax.numpy as jnp
from jax import lax
from jax.experimental import pallas as pl
from jax.experimental.pallas import tpu as pltpu
from jax.sharding import PartitionSpec as P

MESH = pl.DeviceIdType.MESH
LANES = 128
RUNS = 8


def one_minus_exp_neg(u):
    series = 1.0 - u * (1.0 / 8.0)
    for n in (7, 6, 5, 4, 3, 2):
        series = 1.0 - (u * (1.0 / n)) * series
    return jnp.where(u < 0.25, u * series, 1.0 - jnp.exp(-u))


def kernel(
    nz,
    ns,
    taps_ref,
    decay_ref,
    res_ref,
    skip_ref,
    feat_ref,
    out_ref,
    feats,
    tail,
    halo_send,
    halo_recv,
    par_src,
    par_col,
    par_all,
    skip_all,
    wide,
    z_keep,
    g_keep,
    y_keep,
    x_keep,
    e_stage,
    e_recv,
    t_stage,
    t_recv,
    s_stage,
    s_recv,
    o_wide,
    o_keep,
    local_sem,
    pair_send,
    pair_recv,
    tail_sem,
    halo_ssem,
    halo_rsem,
    a_ssem,
    a_rsem,
    k_ssem,
    k_rsem,
    b_ssem,
    b_rsem,
    e_ssem,
    e_rsem,
    t_ssem,
    t_rsem,
    s_ssem,
    s_rsem,
    o_lsem,
    o_ssem,
    o_rsem,
):
    modes = decay_ref.shape[0]
    mp = modes // ns
    rows = feat_ref.shape[1]
    block = 2 * rows
    steps = block // RUNS
    chan = lax.axis_index("chan")
    seq = lax.axis_index("seq")
    z = chan // 2
    k = chan % 2
    other = 1 - k
    position = seq * nz + z
    first = position == 0
    last = position == nz * ns - 1
    f32 = jnp.float32

    def dev(zz, kk, ss):
        return {"chan": zz * 2 + kk, "seq": ss}

    def remote(src, dst, ssem, rsem, device):
        return pltpu.make_async_remote_copy(
            src_ref=src, dst_ref=dst, send_sem=ssem, recv_sem=rsem, device_id=device, device_id_type=MESH
        )

    def local(src, dst, sem):
        return pltpu.make_async_copy(src, dst, sem)

    def wait_bytes(ref, sem):
        pltpu.make_async_copy(ref, ref, sem).wait()

    def far_first(n):
        return (nz // 2 + ((n + 1) // 2) * (1 - 2 * (n % 2))) % nz

    def cols(j, kk):
        return pl.ds(pl.multiple_of((2 * j + kk) * LANES, LANES), LANES)

    my_rows = pl.ds(pl.multiple_of(k * rows, rows), rows)
    other_rows = pl.ds(pl.multiple_of(other * rows, rows), rows)

    barrier = pltpu.get_barrier_semaphore()

    def hello(device):
        pl.semaphore_signal(barrier, inc=1, device_id=device, device_id_type=MESH)

    def hello_z(n, c):
        hello(dev((z + n) % nz, k, seq))
        return c

    def hello_s(n, c):
        hello(dev(z, k, (seq + n) % ns))
        return c

    hello(dev(z, other, seq))
    lax.fori_loop(1, nz, hello_z, 0)
    lax.fori_loop(1, ns, hello_s, 0)
    before = position - 1 + nz * ns
    after = position + 1

    @pl.when(jnp.logical_not(first))
    def _():
        hello(dev(before % nz, 1, (before // nz) % ns))

    sends_halo = jnp.logical_and(k == 1, jnp.logical_not(last))

    def fetch(n, c):
        j = (z + far_first(n)) % nz
        local(feat_ref.at[:, :, cols(j, k)], feats.at[j, :, my_rows, :], local_sem.at[j]).start()
        return c

    @pl.when(sends_halo)
    def _():
        local(feat_ref.at[:, pl.ds(rows - 16, 16), :], tail, tail_sem).start()

    lax.fori_loop(0, nz, fetch, 0)

    decay = decay_ref[...]
    base = jnp.exp(-decay)
    weight = res_ref[...] * jnp.sqrt(one_minus_exp_neg(2.0 * decay))
    for m in range(modes):
        par_src[m, 0:1, :] = base[m : m + 1, :]
        par_src[m, 1:2, :] = weight[m : m + 1, :]

    pl.semaphore_wait(barrier, (nz - 1) + (ns - 1) + 1 + 2 * sends_halo.astype(jnp.int32))

    my_modes = par_src.at[pl.ds(seq * mp, mp)]

    def send_a(n, c):
        remote(my_modes, par_col.at[z], a_ssem, a_rsem, dev((z + far_first(n)) % nz, k, seq)).start()
        return c

    lax.fori_loop(0, nz - 1, send_a, 0)
    local(my_modes, par_col.at[z], a_rsem).start()

    def swap(n, c):
        j = (z + far_first(n)) % nz
        remote(
            feat_ref.at[:, :, cols(j, other)],
            feats.at[j, :, my_rows, :],
            pair_send,
            pair_recv.at[j],
            dev(z, other, seq),
        ).start()
        return c

    lax.fori_loop(0, nz, swap, 0)

    def send_k(n, c):
        remote(skip_ref, skip_all.at[z], k_ssem, k_rsem, dev((z + far_first(n)) % nz, k, seq)).start()
        return c

    lax.fori_loop(0, nz - 1, send_k, 0)
    local(skip_ref, skip_all.at[z], k_rsem).start()

    @pl.when(sends_halo)
    def _():
        local(feat_ref.at[:, pl.ds(rows - 16, 16), :], tail, tail_sem).wait()

        def pick(j, c):
            for kk in range(2):
                for p in range(3):
                    wide_tail = tail[p, :, cols(j, kk)].astype(f32)
                    halo_send[kk, j, 2 * p : 2 * p + 2, :] = wide_tail[14:16, :]
            return c

        lax.fori_loop(0, nz, pick, 0)
        for kk in range(2):
            remote(
                halo_send.at[kk], halo_recv, halo_ssem, halo_rsem, dev(after % nz, kk, (after // nz) % ns)
            ).start()

    wait_bytes(par_col, a_rsem)

    def send_b(n, c):
        remote(par_col, par_all.at[seq], b_ssem, b_rsem, dev(z, k, (seq + n) % ns)).start()
        return c

    lax.fori_loop(1, ns, send_b, 0)
    local(par_col, par_all.at[seq], b_rsem).start()

    @pl.when(first)
    def _():
        halo_recv[...] = jnp.zeros_like(halo_recv)

    @pl.when(jnp.logical_not(first))
    def _():
        wait_bytes(halo_recv, halo_rsem)

    wait_bytes(par_all, b_rsem)
    wait_bytes(skip_all, k_rsem)

    row_id = lax.broadcasted_iota(jnp.int32, (RUNS, LANES), 0)

    def shifted(x, by):
        return jnp.where(row_id >= by, pltpu.roll(x, by, axis=0), 0.0)

    def spread(row):
        return jnp.broadcast_to(row, (RUNS, LANES))

    def par(m, j, which):
        return spread(par_all[m // mp, j, m % mp, which : which + 1, :])

    def run_rows(i):
        return pl.ds(i, RUNS, stride=steps)

    def forward(n, c):
        j = (z + far_first(n)) % nz
        local(feat_ref.at[:, :, cols(j, k)], feats.at[j, :, my_rows, :], local_sem.at[j]).wait()
        remote(
            feat_ref.at[:, :, cols(j, other)],
            feats.at[j, :, other_rows, :],
            pair_send,
            pair_recv.at[j],
            dev(z, other, seq),
        ).wait_recv()
        for p in range(3):
            wide[p] = feats[j, p].astype(f32)
        streams = []
        for p in range(3):
            tap = [spread(taps_ref[p, t : t + 1, cols(j, k)]) for t in range(3)]
            own = [wide[p, run_rows(i), :] for i in range(steps)]
            back1 = jnp.where(row_id == 0, spread(halo_recv[j, 2 * p + 1 : 2 * p + 2, :]), pltpu.roll(own[-1], 1, axis=0))
            back2 = jnp.where(row_id == 0, spread(halo_recv[j, 2 * p : 2 * p + 1, :]), pltpu.roll(own[-2], 1, axis=0))
            seen = [back2, back1] + own
            streams.append(
                [tap[0] * seen[i + 2] + tap[1] * seen[i + 1] + tap[2] * seen[i] for i in range(steps)]
            )
        zs = []
        for i in range(steps):
            g_keep[j, i] = streams[0][i].astype(jnp.bfloat16).astype(f32)
            zs.append((streams[1][i] * streams[2][i]).astype(jnp.bfloat16).astype(f32))
            z_keep[j, i] = zs[i]
        for m in range(modes):
            d = par(m, j, 0)
            acc = zs[0]
            for i in range(1, steps):
                acc = acc * d + zs[i]
            q = d
            reach = 1
            while reach < steps:
                q = q * q
                reach *= 2
            for by in (1, 2, 4):
                acc = acc + q * shifted(acc, by)
                q = q * q
            x_keep[j, m * RUNS : (m + 1) * RUNS, :] = acc
        e_stage[j] = x_keep[j, pl.ds(RUNS - 1, modes, stride=RUNS), :]

        @pl.when(n < nz - 1)
        def _():
            remote(e_stage.at[j], e_recv.at[z], e_ssem, e_rsem, dev(j, k, seq)).start()

        @pl.when(n == nz - 1)
        def _():
            local(e_stage.at[j], e_recv.at[z], e_rsem).start()

        return c

    lax.fori_loop(0, nz, forward, 0)

    def inner(n, c):
        j = (z + far_first(n)) % nz
        taps = [None] * steps
        for m in range(modes):
            d = par(m, j, 0)
            v = par(m, j, 1)
            for i in range(steps):
                taps[i] = v if m == 0 else taps[i] + v
                if i < steps - 1:
                    v = v * d
        taps[0] = taps[0] + spread(skip_all[j])
        zs = [z_keep[j, i] for i in range(steps)]
        for i in range(steps):
            total = taps[0] * zs[i]
            for lag in range(1, i + 1):
                total = total + taps[lag] * zs[i - lag]
            y_keep[j, i] = total
        return c

    lax.fori_loop(0, nz // 2, inner, 0)

    wait_bytes(e_recv, e_rsem)
    block_decay = jnp.exp(-decay * float(block))

    def along_z(zz, state):
        s_stage[zz] = state
        return block_decay * state + e_recv[zz]

    t_stage[...] = lax.fori_loop(0, nz, along_z, jnp.zeros_like(decay))

    def send_t(n, c):
        remote(t_stage, t_recv.at[seq], t_ssem, t_rsem, dev(z, k, (seq + n) % ns)).start()
        return c

    lax.fori_loop(1, ns, send_t, 0)
    local(t_stage, t_recv.at[seq], t_rsem).start()

    lax.fori_loop(nz // 2, nz, inner, 0)

    wait_bytes(t_recv, t_rsem)
    seq_decay = jnp.exp(-decay * float(block * nz))

    def along_s(ss, state):
        return jnp.where(ss < seq, seq_decay * state + t_recv[ss], state)

    incoming = lax.fori_loop(0, ns, along_s, jnp.zeros_like(decay))

    def send_s(n, c):
        zz = (z + far_first(n)) % nz
        s_stage[zz] = s_stage[zz] + jnp.exp(-decay * (zz * block).astype(f32)) * incoming

        @pl.when(n < nz - 1)
        def _():
            remote(s_stage.at[zz], s_recv.at[z], s_ssem, s_rsem.at[z], dev(zz, k, seq)).start()

        @pl.when(n == nz - 1)
        def _():
            local(s_stage.at[zz], s_recv.at[z], s_rsem.at[z]).start()

        return c

    lax.fori_loop(0, nz, send_s, 0)

    def finish(n, c):
        j = (z + far_first(nz - 1 - n)) % nz
        wait_bytes(s_recv.at[j], s_rsem.at[j])
        vs, ds = [], []
        for m in range(modes):
            d = par(m, j, 0)
            q = d
            reach = 1
            while reach < steps:
                q = q * q
                reach *= 2
            q2 = q * q
            power = jnp.where(row_id % 2 == 1, q, 1.0)
            power = power * jnp.where(row_id // 2 % 2 == 1, q2, 1.0)
            power = power * jnp.where(row_id // 4 % 2 == 1, q2 * q2, 1.0)
            start = shifted(x_keep[j, m * RUNS : (m + 1) * RUNS, :], 1) + power * spread(s_recv[j, m : m + 1, :])
            vs.append(par(m, j, 1) * d * start)
            ds.append(d)
        for i in range(steps):
            total = y_keep[j, i]
            for m in range(modes):
                total = total + vs[m]
                if i < steps - 1:
                    vs[m] = vs[m] * ds[m]
            o_wide[run_rows(i), :] = g_keep[j, i] * total
        o_keep[j] = o_wide[...].astype(jnp.bfloat16)
        local(o_keep.at[j, my_rows, :], out_ref.at[:, cols(j, k)], o_lsem).start()
        remote(
            o_keep.at[j, other_rows, :], out_ref.at[:, cols(j, k)], o_ssem, o_rsem, dev(z, other, seq)
        ).start()
        return c

    lax.fori_loop(0, nz, finish, 0)

    half = out_ref.at[:, pl.ds(0, nz * LANES)]
    wait_bytes(half, o_lsem)
    wait_bytes(half, o_ssem)
    wait_bytes(half, o_rsem)
    wait_bytes(feat_ref.at[:, :, pl.ds(0, nz * LANES)], pair_send)
    wait_bytes(par_col.at[pl.ds(0, nz - 1)], a_ssem)
    wait_bytes(skip_all.at[pl.ds(0, nz - 1)], k_ssem)
    wait_bytes(par_all.at[pl.ds(0, ns - 1)], b_ssem)
    wait_bytes(e_recv.at[pl.ds(0, nz - 1)], e_ssem)
    wait_bytes(t_recv.at[pl.ds(0, ns - 1)], t_ssem)
    wait_bytes(s_recv.at[pl.ds(0, nz - 1)], s_ssem)

    @pl.when(sends_halo)
    def _():
        wait_bytes(halo_send, halo_ssem)


def per_device(nz, ns, features, short_taps, decay_rates, residues, skip_gain):
    streams, rows, width = features.shape
    modes = decay_rates.shape[0]
    mp = modes // ns
    block = 2 * rows
    steps = block // RUNS
    f32 = jnp.float32
    vmem = pl.BlockSpec(memory_space=pltpu.VMEM)
    anywhere = pl.BlockSpec(memory_space=pl.ANY)
    dma = pltpu.SemaphoreType.DMA
    return pl.pallas_call(
        functools.partial(kernel, nz, ns),
        out_shape=jax.ShapeDtypeStruct((rows, width), jnp.bfloat16),
        in_specs=[vmem, vmem, vmem, vmem, anywhere],
        out_specs=anywhere,
        scratch_shapes=[
            pltpu.VMEM((nz, streams, block, LANES), jnp.bfloat16),
            pltpu.VMEM((streams, 16, width), jnp.bfloat16),
            pltpu.VMEM((2, nz, 8, LANES), f32),
            pltpu.VMEM((nz, 8, LANES), f32),
            pltpu.VMEM((modes, 2, LANES), f32),
            pltpu.VMEM((nz, mp, 2, LANES), f32),
            pltpu.VMEM((ns, nz, mp, 2, LANES), f32),
            pltpu.VMEM((nz, 1, LANES), f32),
            pltpu.VMEM((streams, block, LANES), f32),
            pltpu.VMEM((nz, steps, RUNS, LANES), f32),
            pltpu.VMEM((nz, steps, RUNS, LANES), f32),
            pltpu.VMEM((nz, steps, RUNS, LANES), f32),
            pltpu.VMEM((nz, modes * RUNS, LANES), f32),
            pltpu.VMEM((nz, modes, LANES), f32),
            pltpu.VMEM((nz, modes, LANES), f32),
            pltpu.VMEM((modes, LANES), f32),
            pltpu.VMEM((ns, modes, LANES), f32),
            pltpu.VMEM((nz, modes, LANES), f32),
            pltpu.VMEM((nz, modes, LANES), f32),
            pltpu.VMEM((block, LANES), f32),
            pltpu.VMEM((nz, block, LANES), jnp.bfloat16),
            dma((nz,)),
            dma,
            dma((nz,)),
            dma,
            dma,
            dma,
            dma,
            dma,
            dma,
            dma,
            dma,
            dma,
            dma,
            dma,
            dma,
            dma,
            dma,
            dma((nz,)),
            dma,
            dma,
            dma,
        ],
        compiler_params=pltpu.CompilerParams(
            collective_id=0, has_side_effects=True, vmem_limit_bytes=24 * 1024 * 1024
        ),
        cost_estimate=pl.CostEstimate(flops=40_000_000, bytes_accessed=2_200_000, transcendentals=0),
    )(short_taps, decay_rates, residues, skip_gain.reshape(1, -1), features)


def solution(mesh):
    nz, ns = mesh.shape["chan"] // 2, mesh.shape["seq"]
    placed = (P(None, ("seq", "chan"), None), P(), P(None, "chan"), P(None, "chan"), P("chan"))
    return jax.shard_map(
        functools.partial(per_device, nz, ns),
        mesh=mesh,
        in_specs=placed,
        out_specs=P(("seq", "chan"), None),
        check_vma=False,
    )
```

time: 361 us -> 58.7 us (0.16)
  the two profiles are of different devices: /device:TPU:7 before, /device:TPU:1 now
where the time goes in v1:
time: 58.7 us; the launch traced here: 58.4 us
  Pallas kernels  53.2 us (91%)
  local copies, waits for them, and re-layouts  5.18 us (9%)
    pallas_call x1, Pallas kernels, per_device(): pl.pallas_call(functools.partial(kernel, nz, ns), out_shape=jax.ShapeDtyp...  53.2 us
    unnamed x11, local copies, waits for them, and re-layouts  5.18 us

profile of v1, /device:TPU:1, one launch (start us, length us, event | category | flops | bytes accessed | tf_op | source)
XLA Modules:
  0.0 58.4 jit_solution(3749715200508293691)
XLA Ops:
  0.0 0.0 copy-start
  0.0 1.4 %copy-done = bf16[3,64,4096]{2,1,0:T(8,128)(2,1)S(1)} copy-done((bf16[3,64,4096]{2,1,0:T(8,128)(2,1)S(1)}, bf16[3,64,4096]{2,1,0:T(8,128)(2,1)}, u32[]{:S(2)}) %copy-start) | copy-done | bytes 1572888
  1.4 0.0 copy-start.1
  1.4 0.9 %copy-done.1 = f32[3,3,4096]{2,1,0:T(4,128)S(1)} copy-done((f32[3,3,4096]{2,1,0:T(4,128)S(1)}, f32[3,3,4096]{2,1,0:T(4,128)}, u32[]{:S(2)}) %copy-start.1) | copy-done | bytes 147480
  2.3 0.0 copy-start.2
  2.3 0.7 %copy-done.2 = f32[16,128]{1,0:T(8,128)S(1)} copy-done((f32[16,128]{1,0:T(8,128)S(1)}, f32[16,128]{1,0:T(8,128)}, u32[]{:S(2)}) %copy-start.2) | copy-done | bytes 8216
  3.0 0.0 copy-start.3
  3.0 0.7 %copy-done.3 = f32[16,128]{1,0:T(8,128)S(1)} copy-done((f32[16,128]{1,0:T(8,128)S(1)}, f32[16,128]{1,0:T(8,128)}, u32[]{:S(2)}) %copy-start.3) | copy-done | bytes 8216
  3.7 0.0 copy-start.4
  3.7 0.7 %copy-done.4 = f32[128]{0:T(128)S(1)} copy-done((f32[128]{0:T(128)S(1)}, f32[128]{0:T(128)}, u32[]{:S(2)}) %copy-start.4) | copy-done | bytes 536
  4.4 53.2 %shard_map.55 = bf16[64,4096]{1,0:T(8,128)(2,1)S(1)} custom-call(f32[3,3,4096]{2,1,0:T(4,128)S(1)} %copy-done.1, f32[16,128]{1,0:T(8,128)S(1)} %copy-done.2, f32[16,128]{1,0:T(8,128)S(1)} %copy-done.3, f32[1,128]{1,0:T(1,128)S(1)} %bitcast.1, bf16[3,64,4096]{2,1,0:T(8,128)(2,1)S(1)} %copy-done), custom_call_target="tpu_custom_call" | custom-call | flops 40000000 | bytes 2200000 | tf_op jit(solution)/shard_map/pallas_call | solution.py:416
  57.6 0.8 %copy.7 = bf16[64,4096]{1,0:T(8,128)(2,1)} copy(bf16[64,4096]{1,0:T(8,128)(2,1)S(1)} %shard_map.55) | data formatting | bytes 1048576
Async XLA Ops:
  0.0 1.4 %copy-start = (bf16[3,64,4096]{2,1,0:T(8,128)(2,1)S(1)}, bf16[3,64,4096]{2,1,0:T(8,128)(2,1)}, u32[]{:S(2)}) copy-start(bf16[3,64,4096]{2,1,0:T(8,128)(2,1)} %feat_ref.1) | copy-start | bytes 4718596
  1.4 0.9 %copy-start.1 = (f32[3,3,4096]{2,1,0:T(4,128)S(1)}, f32[3,3,4096]{2,1,0:T(4,128)}, u32[]{:S(2)}) copy-start(f32[3,3,4096]{2,1,0:T(4,128)} %taps_ref.1) | copy-start | bytes 442372
  2.3 0.7 %copy-start.2 = (f32[16,128]{1,0:T(8,128)S(1)}, f32[16,128]{1,0:T(8,128)}, u32[]{:S(2)}) copy-start(f32[16,128]{1,0:T(8,128)} %decay_ref.1) | copy-start | bytes 24580
  3.0 0.7 %copy-start.3 = (f32[16,128]{1,0:T(8,128)S(1)}, f32[16,128]{1,0:T(8,128)}, u32[]{:S(2)}) copy-start(f32[16,128]{1,0:T(8,128)} %res_ref.1) | copy-start | bytes 24580
  3.7 0.7 %copy-start.4 = (f32[128]{0:T(128)S(1)}, f32[128]{0:T(128)}, u32[]{:S(2)}) copy-start(f32[128]{0:T(128)} %param.9) | copy-start | bytes 1540

commit v2 on v1

v2 whole, which is shorter than its diff:
```python
import functools

import jax
import jax.numpy as jnp
import ml_dtypes
import numpy as np
from jax import lax
from jax.experimental import pallas as pl
from jax.experimental.pallas import tpu as pltpu
from jax.sharding import PartitionSpec as P

MESH = pl.DeviceIdType.MESH
LANES = 128
RUNS = 8
TERMS = 12
GROUP = 4


def fixed_matrices(block):
    steps = block // RUNS
    rows = np.arange(block)
    token = steps * (rows % RUNS) + rows // RUNS

    def polys(lag):
        u = 2.0 * lag / block - 1.0
        out = [np.ones_like(u), u]
        while len(out) < TERMS:
            out.append(2.0 * u * out[-1] - out[-2])
        return np.stack(out)

    def parts(x):
        found = []
        for _ in range(3):
            found.append(x.astype(ml_dtypes.bfloat16))
            x = x - found[-1].astype(np.float64)
        return found

    lag = token[:, None] - token[None, :]
    inside = np.where(lag >= 0, polys(np.maximum(lag, 0).astype(np.float64)), 0.0)
    first, second, _ = parts(inside.reshape(TERMS * block, block))
    toeplitz = np.stack([first, second])

    end = np.zeros((16, block))
    end[:TERMS] = polys((block - 1 - token).astype(np.float64))
    first, second, third = parts(end)
    moments = np.stack([np.concatenate([first, third]), np.concatenate([second, 0 * third])])

    reach = np.zeros((block, 16))
    reach[:, :TERMS] = polys((token + 1).astype(np.float64)).T
    first, second, _ = parts(reach)
    none = 0 * first
    cross = np.concatenate([first, first, first, second, second, none, none, none], axis=1)
    return toeplitz, moments, cross


def one_minus_exp_neg(u):
    series = 1.0 - u * (1.0 / 8.0)
    for n in (7, 6, 5, 4, 3, 2):
        series = 1.0 - (u * (1.0 / n)) * series
    return jnp.where(u < 0.25, u * series, 1.0 - jnp.exp(-u))


def kernel(
    nz,
    ns,
    taps_hbm,
    decay_hbm,
    res_hbm,
    skip_hbm,
    toep_hbm,
    mom_hbm,
    cross_hbm,
    feat_ref,
    out_ref,
    taps_ref,
    decay_ref,
    res_ref,
    skip_ref,
    toep_ref,
    mom_ref,
    cross_ref,
    feats,
    tail,
    halo_send,
    halo_recv,
    h_src,
    h_col,
    h_all,
    c_keep,
    wide,
    z_keep,
    g_keep,
    u_keep,
    y_keep,
    e_stage,
    e_recv,
    p_keep,
    t_stage,
    t_recv,
    r_stage,
    r_recv,
    r_flat,
    o_wide,
    o_keep,
    arg_sem,
    local_sem,
    pair_send,
    pair_recv,
    tail_sem,
    halo_ssem,
    halo_rsem,
    a_ssem,
    a_rsem,
    b_ssem,
    b_rsem,
    e_ssem,
    e_rsem,
    t_ssem,
    t_rsem,
    r_ssem,
    r_rsem,
    o_lsem,
    o_ssem,
    o_rsem,
):
    modes = decay_hbm.shape[0]
    share = 16 // ns
    rows = feat_ref.shape[1]
    block = 2 * rows
    steps = block // RUNS
    chan = lax.axis_index("chan")
    seq = lax.axis_index("seq")
    z = chan // 2
    k = chan % 2
    other = 1 - k
    position = seq * nz + z
    first = position == 0
    last = position == nz * ns - 1
    f32 = jnp.float32

    def dev(zz, kk, ss):
        return {"chan": zz * 2 + kk, "seq": ss}

    def remote(src, dst, ssem, rsem, device):
        return pltpu.make_async_remote_copy(
            src_ref=src, dst_ref=dst, send_sem=ssem, recv_sem=rsem, device_id=device, device_id_type=MESH
        )

    def local(src, dst, sem):
        return pltpu.make_async_copy(src, dst, sem)

    def wait_bytes(ref, sem):
        pltpu.make_async_copy(ref, ref, sem).wait()

    def far_first(n, of=nz):
        return (of // 2 + ((n + 1) // 2) * (1 - 2 * (n % 2))) % of

    def cols(j, kk):
        return pl.ds(pl.multiple_of((2 * j + kk) * LANES, LANES), LANES)

    my_rows = pl.ds(pl.multiple_of(k * rows, rows), rows)
    other_rows = pl.ds(pl.multiple_of(other * rows, rows), rows)

    barrier = pltpu.get_barrier_semaphore()

    def hello(device):
        pl.semaphore_signal(barrier, inc=1, device_id=device, device_id_type=MESH)

    def hello_z(n, c):
        hello(dev((z + far_first(n)) % nz, k, seq))
        return c

    def hello_s(n, c):
        hello(dev(z, k, (seq + n) % ns))
        return c

    lax.fori_loop(0, nz - 1, hello_z, 0)
    lax.fori_loop(1, ns, hello_s, 0)
    hello(dev(z, other, seq))
    before = position - 1 + nz * ns
    after = position + 1

    @pl.when(jnp.logical_not(first))
    def _():
        hello(dev(before % nz, 1, (before // nz) % ns))

    sends_halo = jnp.logical_and(k == 1, jnp.logical_not(last))

    def fetch(n, c):
        j = (z + far_first(n)) % nz
        local(feat_ref.at[:, :, cols(j, k)], feats.at[j, :, my_rows, :], local_sem.at[j]).start()
        return c

    left, right = slice(0, block), slice(block, 2 * block)
    smalls = [
        (decay_hbm, decay_ref),
        (res_hbm, res_ref),
        (skip_hbm, skip_ref),
        (taps_hbm, taps_ref),
        (mom_hbm.at[0], mom_ref.at[:, left]),
        (mom_hbm.at[1], mom_ref.at[:, right]),
        (toep_hbm.at[0], toep_ref.at[:, left]),
        (toep_hbm.at[1], toep_ref.at[:, right]),
        (cross_hbm, cross_ref),
    ]

    def ready(numbers):
        for i in numbers:
            local(*smalls[i], arg_sem.at[i]).wait()

    for i, (src, dst) in enumerate(smalls[:3]):
        local(src, dst, arg_sem.at[i]).start()

    @pl.when(sends_halo)
    def _():
        local(feat_ref.at[:, pl.ds(rows - 16, 16), :], tail, tail_sem).start()

    lax.fori_loop(0, nz, fetch, 0)
    for i, (src, dst) in enumerate(smalls[3:]):
        local(src, dst, arg_sem.at[3 + i]).start()

    ready((0, 1, 2))
    decay = decay_ref[...]
    weight = res_ref[...] * jnp.sqrt(one_minus_exp_neg(2.0 * decay))
    half_a = decay * (block / 4.0)
    square = half_a * half_a
    lead = jnp.exp(-2.0 * half_a)
    for t in range(TERMS):
        total = jnp.ones_like(square)
        for i in range(10, 0, -1):
            total = 1.0 + square * (1.0 / (i * (i + t))) * total
        coef = lead * total * (1.0 if t == 0 else 2.0)
        lead = lead * half_a * (-1.0 / (t + 1))
        c_keep[0, t] = coef
        c_keep[1, t] = weight * coef
        h_src[t] = jnp.sum(weight * coef, axis=0, keepdims=True)
    for t in range(TERMS, 16):
        h_src[t] = skip_ref[...]
    r_flat[...] = jnp.zeros_like(r_flat)

    @pl.when(sends_halo)
    def _():
        local(feat_ref.at[:, pl.ds(rows - 16, 16), :], tail, tail_sem).wait()

        def pick(j, c):
            for kk in range(2):
                for q in range(3):
                    wide_tail = tail[q, :, cols(j, kk)].astype(f32)
                    halo_send[kk, j, q] = wide_tail[14:16, :]
            return c

        lax.fori_loop(0, nz, pick, 0)

    pl.semaphore_wait(barrier, (nz - 1) + (ns - 1) + 1 + 2 * sends_halo.astype(jnp.int32))

    @pl.when(sends_halo)
    def _():
        for kk in range(2):
            remote(
                halo_send.at[kk], halo_recv, halo_ssem, halo_rsem, dev(after % nz, kk, (after // nz) % ns)
            ).start()

    def swap(n, c):
        j = (z + far_first(n)) % nz
        remote(
            feat_ref.at[:, :, cols(j, other)],
            feats.at[j, :, my_rows, :],
            pair_send,
            pair_recv.at[j],
            dev(z, other, seq),
        ).start()
        return c

    lax.fori_loop(0, nz, swap, 0)

    my_rows_h = h_src.at[pl.ds(seq * share, share)]

    def send_a(n, c):
        remote(my_rows_h, h_col.at[z], a_ssem, a_rsem, dev((z + far_first(n)) % nz, k, seq)).start()
        return c

    lax.fori_loop(0, nz - 1, send_a, 0)
    local(my_rows_h, h_col.at[z], a_rsem).start()

    @pl.when(first)
    def _():
        halo_recv[...] = jnp.zeros_like(halo_recv)

    @pl.when(jnp.logical_not(first))
    def _():
        wait_bytes(halo_recv, halo_rsem)

    ready((3, 4, 5))

    row_id = lax.broadcasted_iota(jnp.int32, (RUNS, LANES), 0)

    def spread(row):
        return jnp.broadcast_to(row, (RUNS, LANES))

    def run_rows(i):
        return pl.ds(i, RUNS, stride=steps)

    def term(ref, j, t):
        return ref[j, t // GROUP, t % GROUP : t % GROUP + 1, :]

    def conv(j, p, lanes):
        local(feat_ref.at[:, :, cols(j, k)], feats.at[j, :, my_rows, :], local_sem.at[j]).wait()
        remote(
            feat_ref.at[:, :, cols(j, other)],
            feats.at[j, :, other_rows, :],
            pair_send,
            pair_recv.at[j],
            dev(z, other, seq),
        ).wait_recv()
        for q in range(3):
            wide[q] = feats[j, q].astype(f32)
        streams = []
        for q in range(3):
            tap = [spread(taps_ref[q, t : t + 1, cols(j, k)]) for t in range(3)]
            own = [wide[q, run_rows(i), :] for i in range(steps)]
            back1 = jnp.where(row_id == 0, spread(halo_recv[j, q, 1:2, :]), pltpu.roll(own[-1], 1, axis=0))
            back2 = jnp.where(row_id == 0, spread(halo_recv[j, q, 0:1, :]), pltpu.roll(own[-2], 1, axis=0))
            seen = [back2, back1] + own
            streams.append(
                [tap[0] * seen[i + 2] + tap[1] * seen[i + 1] + tap[2] * seen[i] for i in range(steps)]
            )
        for i in range(steps):
            g_keep[j, i * RUNS : (i + 1) * RUNS, :] = streams[0][i].astype(jnp.bfloat16).astype(f32)
        product = jnp.concatenate([streams[1][i] * streams[2][i] for i in range(steps)], axis=0).astype(jnp.bfloat16)
        z_keep[p, 0:block, lanes] = product
        z_keep[p, block : 2 * block, lanes] = product

    def forward(n, c):
        p = (z // 2 + far_first(n, nz // 2)) % (nz // 2)
        for h in range(2):
            conv(2 * p + h, p, pl.ds(h * LANES, LANES))
        found = jnp.dot(mom_ref[...], z_keep[p], preferred_element_type=f32)
        found = found[0:16] + found[16:32]
        for h in range(2):
            j = 2 * p + h
            for a in range(TERMS // GROUP):
                e_stage[j, a] = found[a * GROUP : (a + 1) * GROUP, h * LANES : (h + 1) * LANES]

            @pl.when(j != z)
            def _():
                remote(e_stage.at[j], e_recv.at[z], e_ssem, e_rsem, dev(j, k, seq)).start()

            @pl.when(j == z)
            def _():
                local(e_stage.at[j], e_recv.at[z], e_rsem).start()

        return c

    lax.fori_loop(0, nz // 2, forward, 0)

    def inner(p, c):
        u_keep[...] = jnp.dot(toep_ref[...], z_keep[p], preferred_element_type=f32)
        for h in range(2):
            j = 2 * p + h
            lanes = slice(h * LANES, (h + 1) * LANES)
            hs = [spread(h_all[t // share, j, t % share]) for t in range(TERMS)]
            skip = spread(h_all[TERMS // share, j, TERMS % share])
            for i in range(0, steps, 2):
                kept = z_keep[p, i * RUNS : (i + 2) * RUNS, lanes].astype(f32)
                for b in range(2):
                    row = (i + b) * RUNS
                    total = skip * kept[b * RUNS : (b + 1) * RUNS]
                    for t in range(TERMS):
                        total = total + hs[t] * u_keep[t * block + row : t * block + row + RUNS, lanes]
                    y_keep[j, row : row + RUNS, :] = total
        return c

    wait_bytes(h_col, a_rsem)

    def send_b(n, c):
        remote(h_col, h_all.at[seq], b_ssem, b_rsem, dev(z, k, (seq + n) % ns)).start()
        return c

    lax.fori_loop(1, ns, send_b, 0)
    local(h_col, h_all.at[seq], b_rsem).start()

    wait_bytes(e_recv, e_rsem)
    block_decay = jnp.exp(-decay * float(block))

    def along_z(zz, state):
        p_keep[zz] = state
        added = c_keep[0, 0] * term(e_recv, zz, 0)
        for t in range(1, TERMS):
            added = added + c_keep[0, t] * term(e_recv, zz, t)
        return block_decay * state + added

    t_stage[...] = lax.fori_loop(0, nz, along_z, jnp.zeros_like(decay))

    def send_t(ss, c):
        remote(t_stage, t_recv.at[seq], t_ssem.at[ss], t_rsem.at[seq], dev(z, k, ss)).start()
        return c

    lax.fori_loop(seq + 1, ns, send_t, 0)

    wait_bytes(h_all, b_rsem)
    ready((6, 7, 8))
    lax.fori_loop(0, nz // 4, inner, 0)

    seq_decay = jnp.exp(-decay * float(block * nz))

    def along_s(ss, state):
        wait_bytes(t_recv.at[ss], t_rsem.at[ss])
        return seq_decay * state + t_recv[ss]

    incoming = lax.fori_loop(0, seq, along_s, jnp.zeros_like(decay))

    def send_r(n, c):
        zz = (z + far_first(n)) % nz
        state = p_keep[zz] + jnp.exp(-decay * (zz * block).astype(f32)) * incoming
        for t in range(TERMS):
            r_stage[zz, t // GROUP, t % GROUP : t % GROUP + 1, :] = jnp.sum(c_keep[1, t] * state, axis=0, keepdims=True)

        @pl.when(n < nz - 1)
        def _():
            remote(r_stage.at[zz], r_recv.at[z], r_ssem, r_rsem.at[z], dev(zz, k, seq)).start()

        @pl.when(n == nz - 1)
        def _():
            local(r_stage.at[zz], r_recv.at[z], r_rsem.at[z]).start()

        return c

    lax.fori_loop(0, nz, send_r, 0)
    lax.fori_loop(nz // 4, nz // 2, inner, 0)

    def finish(n, c):
        p = (z // 2 + far_first(nz // 2 - 1 - n, nz // 2)) % (nz // 2)
        for h in range(2):
            j = 2 * p + h
            wait_bytes(r_recv.at[j], r_rsem.at[j])
            for a in range(TERMS // GROUP):
                r_flat[a * GROUP : (a + 1) * GROUP, h * LANES : (h + 1) * LANES] = r_recv[j, a]
        coef = r_flat[...]
        one = coef.astype(jnp.bfloat16)
        rest = coef - one.astype(f32)
        two = rest.astype(jnp.bfloat16)
        three = (rest - two.astype(f32)).astype(jnp.bfloat16)
        none = jnp.zeros_like(one)
        stacked = jnp.concatenate([one, two, three, one, two, none, none, none], axis=0)
        reached = jnp.dot(cross_ref[...], stacked, preferred_element_type=f32)
        for h in range(2):
            j = 2 * p + h
            for i in range(steps):
                at = slice(i * RUNS, (i + 1) * RUNS)
                o_wide[h, run_rows(i), :] = g_keep[j, at, :] * (
                    y_keep[j, at, :] + reached[at, h * LANES : (h + 1) * LANES]
                )
            o_keep[j] = o_wide[h].astype(jnp.bfloat16)
            local(o_keep.at[j, my_rows, :], out_ref.at[:, cols(j, k)], o_lsem).start()
            remote(
                o_keep.at[j, other_rows, :], out_ref.at[:, cols(j, k)], o_ssem, o_rsem, dev(z, other, seq)
            ).start()
        return c

    lax.fori_loop(0, nz // 2, finish, 0)

    half = out_ref.at[:, pl.ds(0, nz * LANES)]
    wait_bytes(half, o_lsem)
    wait_bytes(half, o_ssem)
    wait_bytes(half, o_rsem)
    wait_bytes(feat_ref.at[:, :, pl.ds(0, nz * LANES)], pair_send)
    wait_bytes(h_col.at[pl.ds(0, nz - 1)], a_ssem)
    wait_bytes(h_all.at[pl.ds(0, ns - 1)], b_ssem)
    wait_bytes(e_recv.at[pl.ds(0, nz - 1)], e_ssem)

    def sent_t(ss, c):
        wait_bytes(t_stage, t_ssem.at[ss])
        return c

    lax.fori_loop(seq + 1, ns, sent_t, 0)
    wait_bytes(r_recv.at[pl.ds(0, nz - 1)], r_ssem)

    @pl.when(sends_halo)
    def _():
        wait_bytes(halo_send, halo_ssem)


def per_device(nz, ns, features, short_taps, decay_rates, residues, skip_gain):
    streams, rows, width = features.shape
    modes = decay_rates.shape[0]
    block = 2 * rows
    groups = TERMS // GROUP
    toeplitz, moments, cross = fixed_matrices(block)
    f32 = jnp.float32
    bf16 = jnp.bfloat16
    hbm = pl.BlockSpec(memory_space=pltpu.HBM)
    anywhere = pl.BlockSpec(memory_space=pl.ANY)
    dma = pltpu.SemaphoreType.DMA
    return pl.pallas_call(
        functools.partial(kernel, nz, ns),
        out_shape=jax.ShapeDtypeStruct((rows, width), jnp.bfloat16),
        in_specs=[hbm] * 8,
        out_specs=anywhere,
        scratch_shapes=[
            pltpu.VMEM(short_taps.shape, f32),
            pltpu.VMEM((modes, LANES), f32),
            pltpu.VMEM((modes, LANES), f32),
            pltpu.VMEM((1, LANES), f32),
            pltpu.VMEM((TERMS * block, 2 * block), bf16),
            pltpu.VMEM((32, 2 * block), bf16),
            pltpu.VMEM(cross.shape, bf16),
            pltpu.VMEM((nz, streams, block, LANES), bf16),
            pltpu.VMEM((streams, 16, width), bf16),
            pltpu.VMEM((2, nz, streams, 2, LANES), f32),
            pltpu.VMEM((nz, streams, 2, LANES), f32),
            pltpu.VMEM((16, 1, LANES), f32),
            pltpu.VMEM((nz, 16 // ns, 1, LANES), f32),
            pltpu.VMEM((ns, nz, 16 // ns, 1, LANES), f32),
            pltpu.VMEM((2, TERMS, modes, LANES), f32),
            pltpu.VMEM((streams, block, LANES), f32),
            pltpu.VMEM((nz // 2, 2 * block, 2 * LANES), bf16),
            pltpu.VMEM((nz, block, LANES), f32),
            pltpu.VMEM((TERMS * block, 2 * LANES), f32),
            pltpu.VMEM((nz, block, LANES), f32),
            pltpu.VMEM((nz, groups, GROUP, LANES), f32),
            pltpu.VMEM((nz, groups, GROUP, LANES), f32),
            pltpu.VMEM((nz, modes, LANES), f32),
            pltpu.VMEM((modes, LANES), f32),
            pltpu.VMEM((ns, modes, LANES), f32),
            pltpu.VMEM((nz, groups, GROUP, LANES), f32),
            pltpu.VMEM((nz, groups, GROUP, LANES), f32),
            pltpu.VMEM((16, 2 * LANES), f32),
            pltpu.VMEM((2, block, LANES), f32),
            pltpu.VMEM((nz, block, LANES), bf16),
            dma((9,)),
            dma((nz,)),
            dma,
            dma((nz,)),
            dma,
            dma,
            dma,
            dma,
            dma,
            dma,
            dma,
            dma,
            dma,
            dma((ns,)),
            dma((ns,)),
            dma,
            dma((nz,)),
            dma,
            dma,
            dma,
        ],
        compiler_params=pltpu.CompilerParams(
            collective_id=0, has_side_effects=True, vmem_limit_bytes=60 * 1024 * 1024
        ),
        cost_estimate=pl.CostEstimate(flops=40_000_000, bytes_accessed=2_200_000, transcendentals=0),
    )(short_taps, decay_rates, residues, skip_gain.reshape(1, -1), toeplitz, moments, cross, features)


def solution(mesh):
    nz, ns = mesh.shape["chan"] // 2, mesh.shape["seq"]
    placed = (P(None, ("seq", "chan"), None), P(), P(None, "chan"), P(None, "chan"), P("chan"))
    return jax.shard_map(
        functools.partial(per_device, nz, ns),
        mesh=mesh,
        in_specs=placed,
        out_specs=P(("seq", "chan"), None),
        check_vma=False,
    )
```

time: 58.7 us -> 43.7 us (0.74)
  the two profiles are of different devices: /device:TPU:1 before, /device:TPU:7 now
where the time goes in v2:
time: 43.7 us; the launch traced here: 43.5 us
  Pallas kernels  41.7 us (95%)
  local copies, waits for them, and re-layouts  1.87 us (4%)
    pallas_call x1, Pallas kernels, per_device(): pl.pallas_call(functools.partial(kernel, nz, ns), out_shape=jax.ShapeDtyp...  41.7 us
    unnamed x1, local copies, waits for them, and re-layouts  1.87 us

profile of v2, /device:TPU:7, one launch (start us, length us, event | category | flops | bytes accessed | tf_op | source)
XLA Modules:
  0.0 43.5 jit_solution(803031747331112510)
XLA Ops:
  0.0 41.7 %shard_map.82 = bf16[64,4096]{1,0:T(8,128)(2,1)} custom-call(f32[3,3,4096]{2,1,0:T(4,128)} %taps_hbm.1, f32[16,128]{1,0:T(8,128)} %decay_hbm.1, f32[16,128]{1,0:T(8,128)} %res_hbm.1, f32[1,128]{1,0:T(1,128)} %bitcast.1, bf16[2,1536,128]{2,1,0:T(8,128)(2,1)} %constant.6.clone.toep_hbm, bf16[2,32,128]{2,1,0:T(8,128)(2,1)} %constant.7.clone.mom_hbm, ...), custom_call_target="tpu_custom_call" | custom-call | flops 40000000 | bytes 2200000 | tf_op jit(solution)/shard_map/pallas_call | solution.py:494
  41.7 1.9 %copy.10 = bf16[64,4096]{1,0:T(8,128)(2,1)} copy(bf16[64,4096]{1,0:T(8,128)(2,1)} %shard_map.82) | data formatting | bytes 1048576

commit v3 on v2

--- a/solution.py
+++ b/solution.py
@@ -13,13 +13,14 @@
 LANES = 128
 RUNS = 8
 TERMS = 12
-GROUP = 4
 
 
 def fixed_matrices(block):
-    steps = block // RUNS
-    rows = np.arange(block)
+    half = block // 2
+    steps = half // RUNS
+    rows = np.arange(half)
     token = steps * (rows % RUNS) + rows // RUNS
+    token = np.concatenate([token, half + token])
 
     def polys(lag):
         u = 2.0 * lag / block - 1.0
@@ -49,7 +50,7 @@
     reach[:, :TERMS] = polys((token + 1).astype(np.float64)).T
     first, second, _ = parts(reach)
     none = 0 * first
-    cross = np.concatenate([first, first, first, second, second, none, none, none], axis=1)
+    cross = np.concatenate([first, second] + [none] * 6, axis=1)
     return toeplitz, moments, cross
 
 
@@ -80,9 +81,12 @@
     mom_ref,
     cross_ref,
     feats,
-    tail,
     halo_send,
     halo_recv,
+    edge_out,
+    edges,
+    z_out,
+    g_out,
     h_src,
     h_col,
     h_all,
@@ -104,9 +108,12 @@
     o_keep,
     arg_sem,
     local_sem,
-    pair_send,
-    pair_recv,
-    tail_sem,
+    z_ssem,
+    z_rsem,
+    g_ssem,
+    g_rsem,
+    edge_ssem,
+    edge_rsem,
     halo_ssem,
     halo_rsem,
     a_ssem,
@@ -127,7 +134,8 @@
     share = 16 // ns
     rows = feat_ref.shape[1]
     block = 2 * rows
-    steps = block // RUNS
+    steps = rows // RUNS
+    pairs = nz // 2
     chan = lax.axis_index("chan")
     seq = lax.axis_index("seq")
     z = chan // 2
@@ -186,17 +194,22 @@
 
     sends_halo = jnp.logical_and(k == 1, jnp.logical_not(last))
 
-    def fetch(n, c):
-        j = (z + far_first(n)) % nz
-        local(feat_ref.at[:, :, cols(j, k)], feats.at[j, :, my_rows, :], local_sem.at[j]).start()
+    wide_cols = 4 * LANES
+
+    def chunk(p):
+        at = pl.ds(pl.multiple_of(p * wide_cols, wide_cols), wide_cols)
+        return local(feat_ref.at[:, :, at], feats.at[p], local_sem.at[p])
+
+    def fetch(p, c):
+        chunk(p).start()
         return c
 
     left, right = slice(0, block), slice(block, 2 * block)
     smalls = [
+        (taps_hbm, taps_ref),
         (decay_hbm, decay_ref),
         (res_hbm, res_ref),
         (skip_hbm, skip_ref),
-        (taps_hbm, taps_ref),
         (mom_hbm.at[0], mom_ref.at[:, left]),
         (mom_hbm.at[1], mom_ref.at[:, right]),
         (toep_hbm.at[0], toep_ref.at[:, left]),
@@ -208,18 +221,56 @@
         for i in numbers:
             local(*smalls[i], arg_sem.at[i]).wait()
 
-    for i, (src, dst) in enumerate(smalls[:3]):
-        local(src, dst, arg_sem.at[i]).start()
-
-    @pl.when(sends_halo)
-    def _():
-        local(feat_ref.at[:, pl.ds(rows - 16, 16), :], tail, tail_sem).start()
-
-    lax.fori_loop(0, nz, fetch, 0)
-    for i, (src, dst) in enumerate(smalls[3:]):
-        local(src, dst, arg_sem.at[3 + i]).start()
-
-    ready((0, 1, 2))
+    local(*smalls[0], arg_sem.at[0]).start()
+    lax.fori_loop(0, pairs, fetch, 0)
+    for i, (src, dst) in enumerate(smalls[1:]):
+        local(src, dst, arg_sem.at[1 + i]).start()
+    ready((0,))
+
+    row_id = lax.broadcasted_iota(jnp.int32, (RUNS, LANES), 0)
+
+    def spread(row):
+        return jnp.broadcast_to(row, (RUNS, LANES))
+
+    def run_rows(i, base=0):
+        return pl.ds(base + i, RUNS, stride=steps)
+
+    def conv(p, c):
+        chunk(p).wait()
+        for h in range(2):
+            j = 2 * p + h
+            for mine in (True, False):
+                kk = k if mine else other
+                at = pl.ds(pl.multiple_of((2 * h + kk) * LANES, LANES), LANES)
+                streams = []
+                for q in range(3):
+                    wide[q] = feats[p, q, :, at].astype(f32)
+                    tap = [spread(taps_ref[q, t : t + 1, cols(j, kk)]) for t in range(3)]
+                    own = [wide[q, run_rows(i), :] for i in range(steps)]
+                    seen = [pltpu.roll(own[-2], 1, axis=0), pltpu.roll(own[-1], 1, axis=0)] + own
+                    streams.append(
+                        [tap[0] * seen[i + 2] + tap[1] * seen[i + 1] + tap[2] * seen[i] for i in range(steps)]
+                    )
+                    ends = [wide[q, 0:2, :], wide[q, rows - 2 : rows, :]]
+                    kept = edges.at[k] if mine else edge_out
+                    kept[j, q, 0:2, :] = ends[0]
+                    kept[j, q, 2:4, :] = ends[1]
+                    halo_send[kk, j, q] = ends[1]
+                gate = jnp.concatenate(streams[0], axis=0).astype(jnp.bfloat16)
+                product = jnp.concatenate([streams[1][i] * streams[2][i] for i in range(steps)], axis=0)
+                product = product.astype(jnp.bfloat16)
+                lanes = pl.ds(h * LANES, LANES)
+                if mine:
+                    z_keep[p, my_rows, lanes] = product
+                    g_keep[j, my_rows, :] = gate
+                else:
+                    z_out[p, :, lanes] = product
+                    g_out[j] = gate
+        return c
+
+    lax.fori_loop(0, pairs, conv, 0)
+
+    ready((1, 2, 3))
     decay = decay_ref[...]
     weight = res_ref[...] * jnp.sqrt(one_minus_exp_neg(2.0 * decay))
     half_a = decay * (block / 4.0)
@@ -238,19 +289,6 @@
         h_src[t] = skip_ref[...]
     r_flat[...] = jnp.zeros_like(r_flat)
 
-    @pl.when(sends_halo)
-    def _():
-        local(feat_ref.at[:, pl.ds(rows - 16, 16), :], tail, tail_sem).wait()
-
-        def pick(j, c):
-            for kk in range(2):
-                for q in range(3):
-                    wide_tail = tail[q, :, cols(j, kk)].astype(f32)
-                    halo_send[kk, j, q] = wide_tail[14:16, :]
-            return c
-
-        lax.fori_loop(0, nz, pick, 0)
-
     pl.semaphore_wait(barrier, (nz - 1) + (ns - 1) + 1 + 2 * sends_halo.astype(jnp.int32))
 
     @pl.when(sends_halo)
@@ -260,18 +298,17 @@
                 halo_send.at[kk], halo_recv, halo_ssem, halo_rsem, dev(after % nz, kk, (after // nz) % ns)
             ).start()
 
+    edge_copy = remote(edge_out, edges.at[k], edge_ssem, edge_rsem, dev(z, other, seq))
+    edge_copy.start()
+
+    def z_copy(p):
+        return remote(z_out.at[p], z_keep.at[p, my_rows, :], z_ssem, z_rsem.at[p], dev(z, other, seq))
+
     def swap(n, c):
-        j = (z + far_first(n)) % nz
-        remote(
-            feat_ref.at[:, :, cols(j, other)],
-            feats.at[j, :, my_rows, :],
-            pair_send,
-            pair_recv.at[j],
-            dev(z, other, seq),
-        ).start()
-        return c
-
-    lax.fori_loop(0, nz, swap, 0)
+        z_copy((z // 2 + far_first(n, pairs)) % pairs).start()
+        return c
+
+    lax.fori_loop(0, pairs, swap, 0)
 
     my_rows_h = h_src.at[pl.ds(seq * share, share)]
 
@@ -281,6 +318,8 @@
 
     lax.fori_loop(0, nz - 1, send_a, 0)
     local(my_rows_h, h_col.at[z], a_rsem).start()
+
+    remote(g_out, g_keep.at[:, my_rows, :], g_ssem, g_rsem, dev(z, other, seq)).start()
 
     @pl.when(first)
     def _():
@@ -290,56 +329,39 @@
     def _():
         wait_bytes(halo_recv, halo_rsem)
 
-    ready((3, 4, 5))
-
-    row_id = lax.broadcasted_iota(jnp.int32, (RUNS, LANES), 0)
-
-    def spread(row):
-        return jnp.broadcast_to(row, (RUNS, LANES))
-
-    def run_rows(i):
-        return pl.ds(i, RUNS, stride=steps)
-
-    def term(ref, j, t):
-        return ref[j, t // GROUP, t % GROUP : t % GROUP + 1, :]
-
-    def conv(j, p, lanes):
-        local(feat_ref.at[:, :, cols(j, k)], feats.at[j, :, my_rows, :], local_sem.at[j]).wait()
-        remote(
-            feat_ref.at[:, :, cols(j, other)],
-            feats.at[j, :, other_rows, :],
-            pair_send,
-            pair_recv.at[j],
-            dev(z, other, seq),
-        ).wait_recv()
-        for q in range(3):
-            wide[q] = feats[j, q].astype(f32)
-        streams = []
-        for q in range(3):
-            tap = [spread(taps_ref[q, t : t + 1, cols(j, k)]) for t in range(3)]
-            own = [wide[q, run_rows(i), :] for i in range(steps)]
-            back1 = jnp.where(row_id == 0, spread(halo_recv[j, q, 1:2, :]), pltpu.roll(own[-1], 1, axis=0))
-            back2 = jnp.where(row_id == 0, spread(halo_recv[j, q, 0:1, :]), pltpu.roll(own[-2], 1, axis=0))
-            seen = [back2, back1] + own
-            streams.append(
-                [tap[0] * seen[i + 2] + tap[1] * seen[i + 1] + tap[2] * seen[i] for i in range(steps)]
-            )
-        for i in range(steps):
-            g_keep[j, i * RUNS : (i + 1) * RUNS, :] = streams[0][i].astype(jnp.bfloat16).astype(f32)
-        product = jnp.concatenate([streams[1][i] * streams[2][i] for i in range(steps)], axis=0).astype(jnp.bfloat16)
-        z_keep[p, 0:block, lanes] = product
-        z_keep[p, block : 2 * block, lanes] = product
+    ready((4, 5))
+    wait_bytes(edge_out, edge_rsem)
+
+    def two_first(q, j, h):
+        now = edges[h, j, q, 0:2, :]
+        past = halo_recv[j, q] if h == 0 else edges[0, j, q, 2:4, :]
+        tap = [taps_ref[q, t : t + 1, cols(j, k)] for t in range(3)]
+        one = tap[0] * now[0:1] + tap[1] * past[1:2] + tap[2] * past[0:1]
+        two = tap[0] * now[1:2] + tap[1] * now[0:1] + tap[2] * past[1:2]
+        return one, two
+
+    tile_row = lax.broadcasted_iota(jnp.int32, (16, LANES), 0)
+
+    def mend(old, one, two):
+        fresh = jnp.where(tile_row == 0, jnp.broadcast_to(one, (16, LANES)), old.astype(f32))
+        fresh = jnp.where(tile_row == RUNS, jnp.broadcast_to(two, (16, LANES)), fresh)
+        return fresh.astype(jnp.bfloat16)
 
     def forward(n, c):
-        p = (z // 2 + far_first(n, nz // 2)) % (nz // 2)
+        p = (z // 2 + far_first(n, pairs)) % pairs
+        wait_bytes(z_out.at[p], z_rsem.at[p])
         for h in range(2):
-            conv(2 * p + h, p, pl.ds(h * LANES, LANES))
-        found = jnp.dot(mom_ref[...], z_keep[p], preferred_element_type=f32)
+            lanes = pl.ds(h * LANES, LANES)
+            for core in range(2):
+                at = pl.ds(core * rows, 16)
+                second, third = two_first(1, 2 * p + h, core), two_first(2, 2 * p + h, core)
+                z_keep[p, at, lanes] = mend(z_keep[p, at, lanes], second[0] * third[0], second[1] * third[1])
+        kept = z_keep[p]
+        found = jnp.dot(mom_ref[...], jnp.concatenate([kept, kept], axis=0), preferred_element_type=f32)
         found = found[0:16] + found[16:32]
         for h in range(2):
             j = 2 * p + h
-            for a in range(TERMS // GROUP):
-                e_stage[j, a] = found[a * GROUP : (a + 1) * GROUP, h * LANES : (h + 1) * LANES]
+            e_stage[j] = found[:, h * LANES : (h + 1) * LANES].astype(jnp.bfloat16)
 
             @pl.when(j != z)
             def _():
@@ -351,16 +373,19 @@
 
         return c
 
-    lax.fori_loop(0, nz // 2, forward, 0)
+    lax.fori_loop(0, pairs, forward, 0)
 
     def inner(p, c):
-        u_keep[...] = jnp.dot(toep_ref[...], z_keep[p], preferred_element_type=f32)
+        kept = z_keep[p]
+        u_keep[...] = jnp.dot(
+            toep_ref[...], jnp.concatenate([kept, kept], axis=0), preferred_element_type=f32
+        )
         for h in range(2):
             j = 2 * p + h
             lanes = slice(h * LANES, (h + 1) * LANES)
             hs = [spread(h_all[t // share, j, t % share]) for t in range(TERMS)]
             skip = spread(h_all[TERMS // share, j, TERMS % share])
-            for i in range(0, steps, 2):
+            for i in range(0, 2 * steps, 2):
                 kept = z_keep[p, i * RUNS : (i + 2) * RUNS, lanes].astype(f32)
                 for b in range(2):
                     row = (i + b) * RUNS
@@ -384,12 +409,13 @@
 
     def along_z(zz, state):
         p_keep[zz] = state
-        added = c_keep[0, 0] * term(e_recv, zz, 0)
+        got = e_recv[zz].astype(f32)
+        added = c_keep[0, 0] * got[0:1]
         for t in range(1, TERMS):
-            added = added + c_keep[0, t] * term(e_recv, zz, t)
+            added = added + c_keep[0, t] * got[t : t + 1]
         return block_decay * state + added
 
-    t_stage[...] = lax.fori_loop(0, nz, along_z, jnp.zeros_like(decay))
+    t_stage[...] = lax.fori_loop(0, nz, along_z, jnp.zeros_like(decay)).astype(jnp.bfloat16)
 
     def send_t(ss, c):
         remote(t_stage, t_recv.at[seq], t_ssem.at[ss], t_rsem.at[seq], dev(z, k, ss)).start()
@@ -405,7 +431,7 @@
 
     def along_s(ss, state):
         wait_bytes(t_recv.at[ss], t_rsem.at[ss])
-        return seq_decay * state + t_recv[ss]
+        return seq_decay * state + t_recv[ss].astype(f32)
 
     incoming = lax.fori_loop(0, seq, along_s, jnp.zeros_like(decay))
 
@@ -413,7 +439,8 @@
         zz = (z + far_first(n)) % nz
         state = p_keep[zz] + jnp.exp(-decay * (zz * block).astype(f32)) * incoming
         for t in range(TERMS):
-            r_stage[zz, t // GROUP, t % GROUP : t % GROUP + 1, :] = jnp.sum(c_keep[1, t] * state, axis=0, keepdims=True)
+            r_flat[t : t + 1, :] = jnp.sum(c_keep[1, t] * state, axis=0, keepdims=True)
+        r_stage[zz] = r_flat[...].astype(jnp.bfloat16)
 
         @pl.when(n < nz - 1)
         def _():
@@ -426,30 +453,31 @@
         return c
 
     lax.fori_loop(0, nz, send_r, 0)
-    lax.fori_loop(nz // 4, nz // 2, inner, 0)
+    lax.fori_loop(nz // 4, pairs, inner, 0)
 
     def finish(n, c):
-        p = (z // 2 + far_first(nz // 2 - 1 - n, nz // 2)) % (nz // 2)
+        p = (z // 2 + far_first(pairs - 1 - n, pairs)) % (pairs)
         for h in range(2):
             j = 2 * p + h
             wait_bytes(r_recv.at[j], r_rsem.at[j])
-            for a in range(TERMS // GROUP):
-                r_flat[a * GROUP : (a + 1) * GROUP, h * LANES : (h + 1) * LANES] = r_recv[j, a]
-        coef = r_flat[...]
-        one = coef.astype(jnp.bfloat16)
-        rest = coef - one.astype(f32)
-        two = rest.astype(jnp.bfloat16)
-        three = (rest - two.astype(f32)).astype(jnp.bfloat16)
-        none = jnp.zeros_like(one)
-        stacked = jnp.concatenate([one, two, three, one, two, none, none, none], axis=0)
+        coef = jnp.concatenate([r_recv[2 * p], r_recv[2 * p + 1]], axis=1)
+        none = jnp.zeros_like(coef)
+        stacked = jnp.concatenate([coef, coef] + [none] * 6, axis=0)
         reached = jnp.dot(cross_ref[...], stacked, preferred_element_type=f32)
         for h in range(2):
             j = 2 * p + h
-            for i in range(steps):
-                at = slice(i * RUNS, (i + 1) * RUNS)
-                o_wide[h, run_rows(i), :] = g_keep[j, at, :] * (
-                    y_keep[j, at, :] + reached[at, h * LANES : (h + 1) * LANES]
-                )
+            for core in range(2):
+                at = pl.ds(core * rows, 16)
+                one, two = two_first(0, j, core)
+                g_keep[j, at, :] = mend(g_keep[j, at, :], one, two)
+            for i in range(0, 2 * steps, 2):
+                gate = g_keep[j, i * RUNS : (i + 2) * RUNS, :].astype(f32)
+                for b in range(2):
+                    at = slice((i + b) * RUNS, (i + b + 1) * RUNS)
+                    half, step = (i + b) // steps, (i + b) % steps
+                    o_wide[h, run_rows(step, half * rows), :] = gate[b * RUNS : (b + 1) * RUNS] * (
+                        y_keep[j, at, :] + reached[at, h * LANES : (h + 1) * LANES]
+                    )
             o_keep[j] = o_wide[h].astype(jnp.bfloat16)
             local(o_keep.at[j, my_rows, :], out_ref.at[:, cols(j, k)], o_lsem).start()
             remote(
@@ -457,13 +485,16 @@
             ).start()
         return c
 
-    lax.fori_loop(0, nz // 2, finish, 0)
+    wait_bytes(g_out, g_rsem)
+    lax.fori_loop(0, pairs, finish, 0)
 
     half = out_ref.at[:, pl.ds(0, nz * LANES)]
     wait_bytes(half, o_lsem)
     wait_bytes(half, o_ssem)
     wait_bytes(half, o_rsem)
-    wait_bytes(feat_ref.at[:, :, pl.ds(0, nz * LANES)], pair_send)
+    wait_bytes(z_out, z_ssem)
+    wait_bytes(g_out, g_ssem)
+    wait_bytes(edge_out, edge_ssem)
     wait_bytes(h_col.at[pl.ds(0, nz - 1)], a_ssem)
     wait_bytes(h_all.at[pl.ds(0, ns - 1)], b_ssem)
     wait_bytes(e_recv.at[pl.ds(0, nz - 1)], e_ssem)
@@ -484,7 +515,7 @@
     streams, rows, width = features.shape
     modes = decay_rates.shape[0]
     block = 2 * rows
-    groups = TERMS // GROUP
+    pairs = nz // 2
     toeplitz, moments, cross = fixed_matrices(block)
     f32 = jnp.float32
     bf16 = jnp.bfloat16
@@ -504,33 +535,39 @@
             pltpu.VMEM((TERMS * block, 2 * block), bf16),
             pltpu.VMEM((32, 2 * block), bf16),
             pltpu.VMEM(cross.shape, bf16),
-            pltpu.VMEM((nz, streams, block, LANES), bf16),
-            pltpu.VMEM((streams, 16, width), bf16),
+            pltpu.VMEM((pairs, streams, rows, 4 * LANES), bf16),
             pltpu.VMEM((2, nz, streams, 2, LANES), f32),
             pltpu.VMEM((nz, streams, 2, LANES), f32),
+            pltpu.VMEM((nz, streams, 4, LANES), f32),
+            pltpu.VMEM((2, nz, streams, 4, LANES), f32),
+            pltpu.VMEM((pairs, rows, 2 * LANES), bf16),
+            pltpu.VMEM((nz, rows, LANES), bf16),
             pltpu.VMEM((16, 1, LANES), f32),
             pltpu.VMEM((nz, 16 // ns, 1, LANES), f32),
             pltpu.VMEM((ns, nz, 16 // ns, 1, LANES), f32),
             pltpu.VMEM((2, TERMS, modes, LANES), f32),
-            pltpu.VMEM((streams, block, LANES), f32),
-            pltpu.VMEM((nz // 2, 2 * block, 2 * LANES), bf16),
-            pltpu.VMEM((nz, block, LANES), f32),
+            pltpu.VMEM((streams, rows, LANES), f32),
+            pltpu.VMEM((pairs, block, 2 * LANES), bf16),
+            pltpu.VMEM((nz, block, LANES), bf16),
             pltpu.VMEM((TERMS * block, 2 * LANES), f32),
             pltpu.VMEM((nz, block, LANES), f32),
-            pltpu.VMEM((nz, groups, GROUP, LANES), f32),
-            pltpu.VMEM((nz, groups, GROUP, LANES), f32),
+            pltpu.VMEM((nz, 16, LANES), bf16),
+            pltpu.VMEM((nz, 16, LANES), bf16),
             pltpu.VMEM((nz, modes, LANES), f32),
-            pltpu.VMEM((modes, LANES), f32),
-            pltpu.VMEM((ns, modes, LANES), f32),
-            pltpu.VMEM((nz, groups, GROUP, LANES), f32),
-            pltpu.VMEM((nz, groups, GROUP, LANES), f32),
-            pltpu.VMEM((16, 2 * LANES), f32),
+            pltpu.VMEM((modes, LANES), bf16),
+            pltpu.VMEM((ns, modes, LANES), bf16),
+            pltpu.VMEM((nz, 16, LANES), bf16),
+            pltpu.VMEM((nz, 16, LANES), bf16),
+            pltpu.VMEM((16, LANES), f32),
             pltpu.VMEM((2, block, LANES), f32),
             pltpu.VMEM((nz, block, LANES), bf16),
             dma((9,)),
-            dma((nz,)),
-            dma,
-            dma((nz,)),
+            dma((pairs,)),
+            dma,
+            dma((pairs,)),
+            dma,
+            dma,
+            dma,
             dma,
             dma,
             dma,

time: 43.7 us -> 43.1 us (0.986)
  the two profiles are of different devices: /device:TPU:7 before, /device:TPU:1 now
where the time goes in v3:
time: 43.1 us; the launch traced here: 42.9 us
  Pallas kernels  41 us (95%)
  local copies, waits for them, and re-layouts  1.87 us (4%)
    pallas_call x1, Pallas kernels, per_device(): pl.pallas_call(functools.partial(kernel, nz, ns), out_shape=jax.ShapeDtyp...  41 us
    unnamed x1, local copies, waits for them, and re-layouts  1.87 us

profile of v3, /device:TPU:1, one launch (start us, length us, event | category | flops | bytes accessed | tf_op | source)
XLA Modules:
  0.0 42.9 jit_solution(10983727504964813759)
XLA Ops:
  0.0 41.0 %shard_map.82 = bf16[64,4096]{1,0:T(8,128)(2,1)} custom-call(f32[3,3,4096]{2,1,0:T(4,128)} %taps_hbm.1, f32[16,128]{1,0:T(8,128)} %decay_hbm.1, f32[16,128]{1,0:T(8,128)} %res_hbm.1, f32[1,128]{1,0:T(1,128)} %bitcast.1, bf16[2,1536,128]{2,1,0:T(8,128)(2,1)} %constant.6.clone.toep_hbm, bf16[2,32,128]{2,1,0:T(8,128)(2,1)} %constant.7.clone.mom_hbm, ...), custom_call_target="tpu_custom_call" | custom-call | flops 40000000 | bytes 2200000 | tf_op jit(solution)/shard_map/pallas_call | solution.py:525
  41.1 1.9 %copy.10 = bf16[64,4096]{1,0:T(8,128)(2,1)} copy(bf16[64,4096]{1,0:T(8,128)(2,1)} %shard_map.82) | data formatting | bytes 1048576

commit v4 on v3

--- a/solution.py
+++ b/solution.py
@@ -81,8 +81,10 @@
     mom_ref,
     cross_ref,
     feats,
+    halo_wide,
     halo_send,
     halo_recv,
+    halo_past,
     edge_out,
     edges,
     z_out,
@@ -174,16 +176,10 @@
     def hello(device):
         pl.semaphore_signal(barrier, inc=1, device_id=device, device_id_type=MESH)
 
-    def hello_z(n, c):
+    for n in range(nz - 1):
         hello(dev((z + far_first(n)) % nz, k, seq))
-        return c
-
-    def hello_s(n, c):
+    for n in range(1, ns):
         hello(dev(z, k, (seq + n) % ns))
-        return c
-
-    lax.fori_loop(0, nz - 1, hello_z, 0)
-    lax.fori_loop(1, ns, hello_s, 0)
     hello(dev(z, other, seq))
     before = position - 1 + nz * ns
     after = position + 1
@@ -255,7 +251,7 @@
                     kept = edges.at[k] if mine else edge_out
                     kept[j, q, 0:2, :] = ends[0]
                     kept[j, q, 2:4, :] = ends[1]
-                    halo_send[kk, j, q] = ends[1]
+                    halo_wide[kk, pl.ds(j * 6 + 2 * q, 2), :] = ends[1]
                 gate = jnp.concatenate(streams[0], axis=0).astype(jnp.bfloat16)
                 product = jnp.concatenate([streams[1][i] * streams[2][i] for i in range(steps)], axis=0)
                 product = product.astype(jnp.bfloat16)
@@ -269,6 +265,7 @@
         return c
 
     lax.fori_loop(0, pairs, conv, 0)
+    halo_send[...] = halo_wide[...].astype(jnp.bfloat16)
 
     ready((1, 2, 3))
     decay = decay_ref[...]
@@ -323,18 +320,19 @@
 
     @pl.when(first)
     def _():
-        halo_recv[...] = jnp.zeros_like(halo_recv)
+        halo_past[...] = jnp.zeros_like(halo_past)
 
     @pl.when(jnp.logical_not(first))
     def _():
         wait_bytes(halo_recv, halo_rsem)
+        halo_past[...] = halo_recv[...].astype(f32)
 
     ready((4, 5))
     wait_bytes(edge_out, edge_rsem)
 
     def two_first(q, j, h):
         now = edges[h, j, q, 0:2, :]
-        past = halo_recv[j, q] if h == 0 else edges[0, j, q, 2:4, :]
+        past = halo_past[pl.ds(j * 6 + 2 * q, 2), :] if h == 0 else edges[0, j, q, 2:4, :]
         tap = [taps_ref[q, t : t + 1, cols(j, k)] for t in range(3)]
         one = tap[0] * now[0:1] + tap[1] * past[1:2] + tap[2] * past[0:1]
         two = tap[0] * now[1:2] + tap[1] * now[0:1] + tap[2] * past[1:2]
@@ -425,7 +423,8 @@
 
     wait_bytes(h_all, b_rsem)
     ready((6, 7, 8))
-    lax.fori_loop(0, nz // 4, inner, 0)
+    early = jnp.where(seq == 0, 0, nz // 4)
+    lax.fori_loop(0, early, inner, 0)
 
     seq_decay = jnp.exp(-decay * float(block * nz))
 
@@ -453,7 +452,7 @@
         return c
 
     lax.fori_loop(0, nz, send_r, 0)
-    lax.fori_loop(nz // 4, pairs, inner, 0)
+    lax.fori_loop(early, pairs, inner, 0)
 
     def finish(n, c):
         p = (z // 2 + far_first(pairs - 1 - n, pairs)) % (pairs)
@@ -536,8 +535,10 @@
             pltpu.VMEM((32, 2 * block), bf16),
             pltpu.VMEM(cross.shape, bf16),
             pltpu.VMEM((pairs, streams, rows, 4 * LANES), bf16),
-            pltpu.VMEM((2, nz, streams, 2, LANES), f32),
-            pltpu.VMEM((nz, streams, 2, LANES), f32),
+            pltpu.VMEM((2, nz * 2 * streams, LANES), f32),
+            pltpu.VMEM((2, nz * 2 * streams, LANES), bf16),
+            pltpu.VMEM((nz * 2 * streams, LANES), bf16),
+            pltpu.VMEM((nz * 2 * streams, LANES), f32),
             pltpu.VMEM((nz, streams, 4, LANES), f32),
             pltpu.VMEM((2, nz, streams, 4, LANES), f32),
             pltpu.VMEM((pairs, rows, 2 * LANES), bf16),

time: 43.1 us -> 41.5 us (0.963)
  the two profiles are of different devices: /device:TPU:1 before, /device:TPU:7 now
where the time goes in v4:
time: 41.5 us; the launch traced here: 41.3 us
  Pallas kernels  39.4 us (95%)
  local copies, waits for them, and re-layouts  1.87 us (5%)
    pallas_call x1, Pallas kernels, per_device(): pl.pallas_call(functools.partial(kernel, nz, ns), out_shape=jax.ShapeDtyp...  39.4 us
    unnamed x1, local copies, waits for them, and re-layouts  1.87 us

profile of v4, /device:TPU:7, one launch (start us, length us, event | category | flops | bytes accessed | tf_op | source)
XLA Modules:
  0.0 41.3 jit_solution(18218874856377345151)
XLA Ops:
  0.0 39.4 %shard_map.82 = bf16[64,4096]{1,0:T(8,128)(2,1)} custom-call(f32[3,3,4096]{2,1,0:T(4,128)} %taps_hbm.1, f32[16,128]{1,0:T(8,128)} %decay_hbm.1, f32[16,128]{1,0:T(8,128)} %res_hbm.1, f32[1,128]{1,0:T(1,128)} %bitcast.1, bf16[2,1536,128]{2,1,0:T(8,128)(2,1)} %constant.6.clone.toep_hbm, bf16[2,32,128]{2,1,0:T(8,128)(2,1)} %constant.7.clone.mom_hbm, ...), custom_call_target="tpu_custom_call" | custom-call | flops 40000000 | bytes 2200000 | tf_op jit(solution)/shard_map/pallas_call | solution.py:524
  39.4 1.9 %copy.10 = bf16[64,4096]{1,0:T(8,128)(2,1)} copy(bf16[64,4096]{1,0:T(8,128)(2,1)} %shard_map.82) | data formatting | bytes 1048576

commit v5 on v4

--- a/solution.py
+++ b/solution.py
@@ -421,11 +421,6 @@
 
     lax.fori_loop(seq + 1, ns, send_t, 0)
 
-    wait_bytes(h_all, b_rsem)
-    ready((6, 7, 8))
-    early = jnp.where(seq == 0, 0, nz // 4)
-    lax.fori_loop(0, early, inner, 0)
-
     seq_decay = jnp.exp(-decay * float(block * nz))
 
     def along_s(ss, state):
@@ -452,7 +447,9 @@
         return c
 
     lax.fori_loop(0, nz, send_r, 0)
-    lax.fori_loop(early, pairs, inner, 0)
+    wait_bytes(h_all, b_rsem)
+    ready((6, 7, 8))
+    lax.fori_loop(0, pairs, inner, 0)
 
     def finish(n, c):
         p = (z // 2 + far_first(pairs - 1 - n, pairs)) % (pairs)

time: 41.5 us -> 41.5 us (level)
  no operation moved by 1% of the time
where the time goes in v5:
time: 41.5 us; the launch traced here: 41.3 us
  Pallas kernels  39.4 us (95%)
  local copies, waits for them, and re-layouts  1.87 us (5%)
    pallas_call x1, Pallas kernels, per_device(): pl.pallas_call(functools.partial(kernel, nz, ns), out_shape=jax.ShapeDtyp...  39.4 us
    unnamed x1, local copies, waits for them, and re-layouts  1.87 us

profile of v5, /device:TPU:7, one launch (start us, length us, event | category | flops | bytes accessed | tf_op | source)
XLA Modules:
  0.0 41.3 jit_solution(5112925669725674717)
XLA Ops:
  0.0 39.4 %shard_map.82 = bf16[64,4096]{1,0:T(8,128)(2,1)} custom-call(f32[3,3,4096]{2,1,0:T(4,128)} %taps_hbm.1, f32[16,128]{1,0:T(8,128)} %decay_hbm.1, f32[16,128]{1,0:T(8,128)} %res_hbm.1, f32[1,128]{1,0:T(1,128)} %bitcast.1, bf16[2,1536,128]{2,1,0:T(8,128)(2,1)} %constant.6.clone.toep_hbm, bf16[2,32,128]{2,1,0:T(8,128)(2,1)} %constant.7.clone.mom_hbm, ...), custom_call_target="tpu_custom_call" | custom-call | flops 40000000 | bytes 2200000 | tf_op jit(solution)/shard_map/pallas_call | solution.py:521
  39.4 1.9 %copy.10 = bf16[64,4096]{1,0:T(8,128)(2,1)} copy(bf16[64,4096]{1,0:T(8,128)(2,1)} %shard_map.82) | data formatting | bytes 1048576

commit v6 on v5

--- a/solution.py
+++ b/solution.py
@@ -202,7 +202,7 @@
 
     left, right = slice(0, block), slice(block, 2 * block)
     smalls = [
-        (taps_hbm, taps_ref),
+        (taps_hbm, taps_ref.at[pl.ds(0, 3)]),
         (decay_hbm, decay_ref),
         (res_hbm, res_ref),
         (skip_hbm, skip_ref),
@@ -265,7 +265,7 @@
         return c
 
     lax.fori_loop(0, pairs, conv, 0)
-    halo_send[...] = halo_wide[...].astype(jnp.bfloat16)
+    halo_send[...] = halo_wide[:, 0 : 6 * nz, :].astype(jnp.bfloat16)
 
     ready((1, 2, 3))
     decay = decay_ref[...]
@@ -295,7 +295,7 @@
                 halo_send.at[kk], halo_recv, halo_ssem, halo_rsem, dev(after % nz, kk, (after // nz) % ns)
             ).start()
 
-    edge_copy = remote(edge_out, edges.at[k], edge_ssem, edge_rsem, dev(z, other, seq))
+    edge_copy = remote(edge_out.at[pl.ds(0, nz)], edges.at[k], edge_ssem, edge_rsem, dev(z, other, seq))
     edge_copy.start()
 
     def z_copy(p):
@@ -325,10 +325,10 @@
     @pl.when(jnp.logical_not(first))
     def _():
         wait_bytes(halo_recv, halo_rsem)
-        halo_past[...] = halo_recv[...].astype(f32)
+        halo_past[0 : 6 * nz, :] = halo_recv[...].astype(f32)
 
     ready((4, 5))
-    wait_bytes(edge_out, edge_rsem)
+    wait_bytes(edge_out.at[pl.ds(0, nz)], edge_rsem)
 
     def two_first(q, j, h):
         now = edges[h, j, q, 0:2, :]
@@ -490,7 +490,7 @@
     wait_bytes(half, o_rsem)
     wait_bytes(z_out, z_ssem)
     wait_bytes(g_out, g_ssem)
-    wait_bytes(edge_out, edge_ssem)
+    wait_bytes(edge_out.at[pl.ds(0, nz)], edge_ssem)
     wait_bytes(h_col.at[pl.ds(0, nz - 1)], a_ssem)
     wait_bytes(h_all.at[pl.ds(0, ns - 1)], b_ssem)
     wait_bytes(e_recv.at[pl.ds(0, nz - 1)], e_ssem)
@@ -524,7 +524,7 @@
         in_specs=[hbm] * 8,
         out_specs=anywhere,
         scratch_shapes=[
-            pltpu.VMEM(short_taps.shape, f32),
+            pltpu.VMEM((4,) + short_taps.shape[1:], f32),
             pltpu.VMEM((modes, LANES), f32),
             pltpu.VMEM((modes, LANES), f32),
             pltpu.VMEM((1, LANES), f32),
@@ -532,19 +532,19 @@
             pltpu.VMEM((32, 2 * block), bf16),
             pltpu.VMEM(cross.shape, bf16),
             pltpu.VMEM((pairs, streams, rows, 4 * LANES), bf16),
-            pltpu.VMEM((2, nz * 2 * streams, LANES), f32),
+            pltpu.VMEM((2, nz * 2 * streams + 16, LANES), f32),
             pltpu.VMEM((2, nz * 2 * streams, LANES), bf16),
             pltpu.VMEM((nz * 2 * streams, LANES), bf16),
-            pltpu.VMEM((nz * 2 * streams, LANES), f32),
-            pltpu.VMEM((nz, streams, 4, LANES), f32),
-            pltpu.VMEM((2, nz, streams, 4, LANES), f32),
+            pltpu.VMEM((nz * 2 * streams + 16, LANES), f32),
+            pltpu.VMEM((nz + 1, streams, 4, LANES), f32),
+            pltpu.VMEM((3, nz, streams, 4, LANES), f32),
             pltpu.VMEM((pairs, rows, 2 * LANES), bf16),
             pltpu.VMEM((nz, rows, LANES), bf16),
-            pltpu.VMEM((16, 1, LANES), f32),
+            pltpu.VMEM((24, 1, LANES), f32),
             pltpu.VMEM((nz, 16 // ns, 1, LANES), f32),
             pltpu.VMEM((ns, nz, 16 // ns, 1, LANES), f32),
             pltpu.VMEM((2, TERMS, modes, LANES), f32),
-            pltpu.VMEM((streams, rows, LANES), f32),
+            pltpu.VMEM((streams + 1, rows, LANES), f32),
             pltpu.VMEM((pairs, block, 2 * LANES), bf16),
             pltpu.VMEM((nz, block, LANES), bf16),
             pltpu.VMEM((TERMS * block, 2 * LANES), f32),
@@ -557,7 +557,7 @@
             pltpu.VMEM((nz, 16, LANES), bf16),
             pltpu.VMEM((nz, 16, LANES), bf16),
             pltpu.VMEM((16, LANES), f32),
-            pltpu.VMEM((2, block, LANES), f32),
+            pltpu.VMEM((3, block, LANES), f32),
             pltpu.VMEM((nz, block, LANES), bf16),
             dma((9,)),
             dma((pairs,)),

time: 41.5 us -> 41.5 us (level)
  no operation moved by 1% of the time
where the time goes in v6:
time: 41.5 us; the launch traced here: 41.3 us
  Pallas kernels  39.4 us (95%)
  local copies, waits for them, and re-layouts  1.87 us (5%)
    pallas_call x1, Pallas kernels, per_device(): pl.pallas_call(functools.partial(kernel, nz, ns), out_shape=jax.ShapeDtyp...  39.4 us
    unnamed x1, local copies, waits for them, and re-layouts  1.87 us

profile of v6, /device:TPU:7, one launch (start us, length us, event | category | flops | bytes accessed | tf_op | source)
XLA Modules:
  0.0 41.3 jit_solution(10261498284161400911)
XLA Ops:
  0.0 39.4 %shard_map.82 = bf16[64,4096]{1,0:T(8,128)(2,1)} custom-call(f32[3,3,4096]{2,1,0:T(4,128)} %taps_hbm.1, f32[16,128]{1,0:T(8,128)} %decay_hbm.1, f32[16,128]{1,0:T(8,128)} %res_hbm.1, f32[1,128]{1,0:T(1,128)} %bitcast.1, bf16[2,1536,128]{2,1,0:T(8,128)(2,1)} %constant.6.clone.toep_hbm, bf16[2,32,128]{2,1,0:T(8,128)(2,1)} %constant.7.clone.mom_hbm, ...), custom_call_target="tpu_custom_call" | custom-call | flops 40000000 | bytes 2200000 | tf_op jit(solution)/shard_map/pallas_call | solution.py:521
  39.4 1.9 %copy.10 = bf16[64,4096]{1,0:T(8,128)(2,1)} copy(bf16[64,4096]{1,0:T(8,128)(2,1)} %shard_map.82) | data formatting | bytes 1048576

commit v7 on v6

--- a/solution.py
+++ b/solution.py
@@ -100,6 +100,7 @@
     y_keep,
     e_stage,
     e_recv,
+    a_keep,
     p_keep,
     t_stage,
     t_recv,
@@ -363,11 +364,11 @@
 
             @pl.when(j != z)
             def _():
-                remote(e_stage.at[j], e_recv.at[z], e_ssem, e_rsem, dev(j, k, seq)).start()
+                remote(e_stage.at[j], e_recv.at[z], e_ssem, e_rsem.at[z], dev(j, k, seq)).start()
 
             @pl.when(j == z)
             def _():
-                local(e_stage.at[j], e_recv.at[z], e_rsem).start()
+                local(e_stage.at[j], e_recv.at[z], e_rsem.at[z]).start()
 
         return c
 
@@ -402,16 +403,23 @@
     lax.fori_loop(1, ns, send_b, 0)
     local(h_col, h_all.at[seq], b_rsem).start()
 
-    wait_bytes(e_recv, e_rsem)
     block_decay = jnp.exp(-decay * float(block))
 
-    def along_z(zz, state):
-        p_keep[zz] = state
+    def take(n, c):
+        zz = (z + far_first(nz - 1 - n)) % nz
+        wait_bytes(e_recv.at[zz], e_rsem.at[zz])
         got = e_recv[zz].astype(f32)
         added = c_keep[0, 0] * got[0:1]
         for t in range(1, TERMS):
             added = added + c_keep[0, t] * got[t : t + 1]
-        return block_decay * state + added
+        a_keep[zz] = added
+        return c
+
+    lax.fori_loop(0, nz, take, 0)
+
+    def along_z(zz, state):
+        p_keep[zz] = state
+        return block_decay * state + a_keep[zz]
 
     t_stage[...] = lax.fori_loop(0, nz, along_z, jnp.zeros_like(decay)).astype(jnp.bfloat16)
 
@@ -552,6 +560,7 @@
             pltpu.VMEM((nz, 16, LANES), bf16),
             pltpu.VMEM((nz, 16, LANES), bf16),
             pltpu.VMEM((nz, modes, LANES), f32),
+            pltpu.VMEM((nz, modes, LANES), f32),
             pltpu.VMEM((modes, LANES), bf16),
             pltpu.VMEM((ns, modes, LANES), bf16),
             pltpu.VMEM((nz, 16, LANES), bf16),
@@ -574,7 +583,7 @@
             dma,
             dma,
             dma,
-            dma,
+            dma((nz,)),
             dma((ns,)),
             dma((ns,)),
             dma,

time: 41.5 us -> 41.6 us (level)
  no operation moved by 1% of the time
where the time goes in v7:
time: 41.6 us; the launch traced here: 41.4 us
  Pallas kernels  39.5 us (95%)
  local copies, waits for them, and re-layouts  1.87 us (4%)
    pallas_call x1, Pallas kernels, per_device(): pl.pallas_call(functools.partial(kernel, nz, ns), out_shape=jax.ShapeDtyp...  39.5 us
    unnamed x1, local copies, waits for them, and re-layouts  1.87 us

profile of v7, /device:TPU:7, one launch (start us, length us, event | category | flops | bytes accessed | tf_op | source)
XLA Modules:
  0.0 41.4 jit_solution(15162750112922573088)
XLA Ops:
  0.0 39.5 %shard_map.82 = bf16[64,4096]{1,0:T(8,128)(2,1)} custom-call(f32[3,3,4096]{2,1,0:T(4,128)} %taps_hbm.1, f32[16,128]{1,0:T(8,128)} %decay_hbm.1, f32[16,128]{1,0:T(8,128)} %res_hbm.1, f32[1,128]{1,0:T(1,128)} %bitcast.1, bf16[2,1536,128]{2,1,0:T(8,128)(2,1)} %constant.6.clone.toep_hbm, bf16[2,32,128]{2,1,0:T(8,128)(2,1)} %constant.7.clone.mom_hbm, ...), custom_call_target="tpu_custom_call" | custom-call | flops 40000000 | bytes 2200000 | tf_op jit(solution)/shard_map/pallas_call | solution.py:529
  39.5 1.9 %copy.10 = bf16[64,4096]{1,0:T(8,128)(2,1)} copy(bf16[64,4096]{1,0:T(8,128)(2,1)} %shard_map.82) | data formatting | bytes 1048576

commit v8 on v6

--- a/solution.py
+++ b/solution.py
@@ -380,6 +380,10 @@
         )
         for h in range(2):
             j = 2 * p + h
+            for core in range(2):
+                at = pl.ds(core * rows, 16)
+                one, two = two_first(0, j, core)
+                g_keep[j, at, :] = mend(g_keep[j, at, :], one, two)
             lanes = slice(h * LANES, (h + 1) * LANES)
             hs = [spread(h_all[t // share, j, t % share]) for t in range(TERMS)]
             skip = spread(h_all[TERMS // share, j, TERMS % share])
@@ -448,6 +452,7 @@
 
     lax.fori_loop(0, nz, send_r, 0)
     wait_bytes(h_all, b_rsem)
+    wait_bytes(g_out, g_rsem)
     ready((6, 7, 8))
     lax.fori_loop(0, pairs, inner, 0)
 
@@ -462,10 +467,6 @@
         reached = jnp.dot(cross_ref[...], stacked, preferred_element_type=f32)
         for h in range(2):
             j = 2 * p + h
-            for core in range(2):
-                at = pl.ds(core * rows, 16)
-                one, two = two_first(0, j, core)
-                g_keep[j, at, :] = mend(g_keep[j, at, :], one, two)
             for i in range(0, 2 * steps, 2):
                 gate = g_keep[j, i * RUNS : (i + 2) * RUNS, :].astype(f32)
                 for b in range(2):
@@ -481,7 +482,6 @@
             ).start()
         return c
 
-    wait_bytes(g_out, g_rsem)
     lax.fori_loop(0, pairs, finish, 0)
 
     half = out_ref.at[:, pl.ds(0, nz * LANES)]

time: 41.5 us -> 41.5 us (level)
  no operation moved by 1% of the time
where the time goes in v8:
time: 41.5 us; the launch traced here: 41.3 us
  Pallas kernels  39.4 us (95%)
  local copies, waits for them, and re-layouts  1.87 us (5%)
    pallas_call x1, Pallas kernels, per_device(): pl.pallas_call(functools.partial(kernel, nz, ns), out_shape=jax.ShapeDtyp...  39.4 us
    unnamed x1, local copies, waits for them, and re-layouts  1.87 us

profile of v8, /device:TPU:7, one launch (start us, length us, event | category | flops | bytes accessed | tf_op | source)
XLA Modules:
  0.0 41.3 jit_solution(9820599485535281949)
XLA Ops:
  0.0 39.4 %shard_map.82 = bf16[64,4096]{1,0:T(8,128)(2,1)} custom-call(f32[3,3,4096]{2,1,0:T(4,128)} %taps_hbm.1, f32[16,128]{1,0:T(8,128)} %decay_hbm.1, f32[16,128]{1,0:T(8,128)} %res_hbm.1, f32[1,128]{1,0:T(1,128)} %bitcast.1, bf16[2,1536,128]{2,1,0:T(8,128)(2,1)} %constant.6.clone.toep_hbm, bf16[2,32,128]{2,1,0:T(8,128)(2,1)} %constant.7.clone.mom_hbm, ...), custom_call_target="tpu_custom_call" | custom-call | flops 40000000 | bytes 2200000 | tf_op jit(solution)/shard_map/pallas_call | solution.py:521
  39.4 1.9 %copy.10 = bf16[64,4096]{1,0:T(8,128)(2,1)} copy(bf16[64,4096]{1,0:T(8,128)(2,1)} %shard_map.82) | data formatting | bytes 1048576
